TPU v7x, 256 devices: a whole 4x4x8 slice. The times are simulated.
256 devices in a mesh: dp: 32 (over z, x), tensor: 8 (over y, core).
Axes of the slice: x: 4, y: 4, z: 8, core: 2. Of those that a mesh axis runs over, the one named last changes fastest.
Arguments:
- layer_input: bfloat16 [8192, 512], P('dp'), may hold values from -6 to 6
- output_grad: bfloat16 [8192, 28672], P('dp', 'tensor'), may hold values from -6 to 6
- feedback: bfloat16 [16384, 28672], P('dp', 'tensor'), may hold values from -6 to 6
- basis_prev: float32 [64, 28672], P(None, 'tensor'), may hold values from -6 to 6
Outputs:
- factor_left: float32 [64, 512], replicated
- basis_next: float32 [64, 28672], P(None, 'tensor')
- feedback_next: bfloat16 [16384, 28672], P('dp', 'tensor')
All inputs are finite; a program needn't handle non-finite values.
Results may differ from a plain program's by a relative error of at most 0.0065.
Values sent between devices are 32-bit elements; how exact they have to be, the bound alone decides.
No kernel may reach another device: no remote copies, remote signals or barrier semaphores. Data moves between devices by JAX's collectives and lax.ppermute only.
A program may use at most 64 MiB of HBM per device.

v0:
```python
import math

import jax
import jax.numpy as jnp
from jax import lax
from jax.sharding import PartitionSpec as P


def cholesky_solve(gram_matrix, columns):
    lower_factor = jnp.linalg.cholesky(gram_matrix)
    return jax.scipy.linalg.solve_triangular(lower_factor, columns, lower=True)


def local(layer_input, output_grad, feedback, basis_prev):
    token_count = layer_input.shape[0]
    weight_grad = lax.dot_general(
        layer_input, output_grad, (((0,), (0,)), ((), ())), preferred_element_type=jnp.float32
    )
    weight_grad = weight_grad * (1.0 / math.sqrt(token_count))
    corrected = (weight_grad + feedback.astype(jnp.float32)).astype(jnp.bfloat16)
    basis_low = basis_prev.astype(jnp.bfloat16)
    factor_part = lax.dot_general(
        basis_low, corrected, (((1,), (1,)), ((), ())), preferred_element_type=jnp.float32
    )
    factor_sum = lax.psum(factor_part, ("dp", "tensor"))
    gram_matrix = jnp.dot(factor_sum, factor_sum.T, precision=lax.Precision.HIGHEST)
    factor_left = cholesky_solve(gram_matrix, factor_sum)
    factor_low = factor_left.astype(jnp.bfloat16)
    replica_count = lax.axis_size("dp")
    basis_term = jnp.dot(factor_low, corrected, preferred_element_type=jnp.float32)
    basis_next = lax.psum(basis_term, "dp") / replica_count
    basis_round = basis_next.astype(jnp.bfloat16)
    approx = lax.dot_general(
        factor_low, basis_round, (((0,), (0,)), ((), ())), preferred_element_type=jnp.float32
    )
    feedback_next = (corrected.astype(jnp.float32) - approx).astype(jnp.bfloat16)
    return (factor_left, basis_next, feedback_next)


def solution(mesh):
    in_specs = (P("dp", None), P("dp", "tensor"), P("dp", "tensor"), P(None, "tensor"))
    out_specs = (P(), P(None, "tensor"), P("dp", "tensor"))
    return jax.shard_map(local, mesh=mesh, in_specs=in_specs, out_specs=out_specs, check_vma=False)
```

profile of v0, /device:TPU:64, one launch (start us, length us, event | category | flops | bytes accessed | tf_op | source)
XLA Modules:
  0.0 436.7 jit_solution(18158299209747161578)
XLA Ops:
  7.2 0.0 copy-start
  7.2 0.0 all-reduce.3.cloned.1.call-start
  7.2 1.4 copy-done
  8.7 3.3 add_convert_fusion
  12.0 0.0 copy-start.1
  12.0 1.8 copy-done.1
  13.8 1.9 convolution_bitcast_fusion
  15.7 0.0 all-reduce.3.cloned.1.call-update
  15.7 0.0 all-reduce.5.cloned.1.call-start
  15.8 242.3 %all-reduce.3.cloned.1.call-done = f32[64,512]{1,0:T(8,128)} async-done(((f32[64,512]{1,0:T(8,128)}), f32[64,512]{1,0:T(8,128)}) %all-reduce.3.cloned.1.call-update) | async-done | bytes 131088 | tf_op jit(solution)/shard_map/psum | solution.py:25
  258.1 1.2 fusion.9
  259.3 0.1 copy.7
  259.4 5.8 %cholesky.16 = f32[64,64]{1,0:T(8,128)S(1)} custom-call(f32[64,64]{1,0:T(8,128)S(1)} %fusion.5), custom_call_target="Cholesky" | custom-call | tf_op jit(solution)/shard_map/jit(cholesky)/cholesky | solution.py:10
  265.3 0.6 compare_reduce_fusion
  265.9 0.7 fusion.2
  266.6 4.9 %custom-call.7 = f32[1,64,64]{1,2,0:T(8,128)S(1)} custom-call(f32[1,64,64]{2,1,0:T(8,128)S(1)} %fusion.2), custom_call_target="InvertDiagBlocksLowerTriangular" | custom-call | tf_op jit(solution)/shard_map/jit(_solve_triangular)/triangular_solve | solution.py:11
  271.5 1.2 fusion.3
  272.7 0.0 copy-start.3
  272.7 3.8 fusion.7
  276.5 0.0 all-reduce.5.cloned.1.call-update
  276.5 146.7 %all-reduce.5.cloned.1.call-done = f32[64,3584]{1,0:T(8,128)} async-done(((f32[64,3584]{1,0:T(8,128)}), f32[64,3584]{1,0:T(8,128)}) %all-reduce.5.cloned.1.call-update) | async-done | bytes 917520 | tf_op jit(solution)/shard_map/psum | solution.py:31
  423.3 1.2 broadcast_multiply_fusion
  424.5 0.0 copy-start.2
  424.5 5.3 %subtract_convert_fusion = bf16[512,3584]{1,0:T(8,128)(2,1)} fusion(bf16[512,3584]{1,0:T(8,128)(2,1)} %copy-done.1, f32[64,3584]{1,0:T(8,128)S(1)} %broadcast_multiply_fusion, f32[64,512]{1,0:T(8,128)S(1)} %fusion.3), kind=kOutput, calls=%fused_computation | convolution fusion | flops 240648192 | bytes 8388608 | tf_op jit(solution)/shard_map/dot_general | solution.py:33
  (6 shorter events, 0.0 us)
Async XLA Ops:
  7.2 1.5 copy-start
  7.2 6.6 %copy-start.4 = (f32[64,3584]{1,0:T(8,128)S(1)}, f32[64,3584]{1,0:T(8,128)}, u32[]{:S(2)}) copy-start(f32[64,3584]{1,0:T(8,128)} %param.7) | copy-start | bytes 2752516
  7.2 250.9 %all-reduce.3.cloned.1.call-start = ((), (), s32[]{:S(2)}) async-start(), calls=%async_computation | async-start | bytes 262144 | tf_op jit(solution)/shard_map/psum | solution.py:25
  12.0 1.8 copy-start.1
  15.7 407.6 %all-reduce.5.cloned.1.call-start = ((), (), s32[]{:S(2)}) async-start(), calls=%async_computation.1 | async-start | bytes 1835008 | tf_op jit(solution)/shard_map/psum | solution.py:31
  272.7 151.8 %copy-start.3 = (f32[64,512]{1,0:T(8,128)}, f32[64,512]{1,0:T(8,128)S(1)}, u32[]{:S(2)}) copy-start(f32[64,512]{1,0:T(8,128)S(1)} %fusion.3) | copy-start | bytes 393220
  424.5 5.4 %copy-start.2 = (f32[64,3584]{1,0:T(8,128)}, f32[64,3584]{1,0:T(8,128)S(1)}, u32[]{:S(2)}) copy-start(f32[64,3584]{1,0:T(8,128)S(1)} %broadcast_multiply_fusion) | copy-start | bytes 2752516
Sparse Core Ops, SparseCore 0:
  15.8 242.2 all-reduce.2
  276.7 146.5 all-reduce.4
where the time goes:
time: 439 us; the launch traced here: 437 us
  waiting for transfers between devices  389 us (89%)
  matrix products  16.7 us (4%)
  between operations  14.1 us (3%)
  other arithmetic  13.3 us (3%)
    psum x1, waiting for transfers between devices, local(): factor_sum = lax.psum(factor_part, ('dp', 'tensor'))  242 us
    psum x1, waiting for transfers between devices, local(): basis_next = lax.psum(basis_term, 'dp') / replica_count  147 us
  transfers between devices with their start and end apart: 2, of which 2 were waited for; matrix products, arithmetic and copies ran while one was open for 0% of the time, Pallas kernels for 0%

commit v1 on v0

--- a/solution.py
+++ b/solution.py
@@ -3,7 +3,73 @@
 import jax
 import jax.numpy as jnp
 from jax import lax
+from jax.sharding import Mesh
 from jax.sharding import PartitionSpec as P
+
+SIZES = dict(z=8, x=4, y=4, c=2)
+PLANE = ("x", "y", "c")
+
+
+def group_size(axes):
+    return math.prod(SIZES[a] for a in axes)
+
+
+def shift(block, axis, step):
+    n = SIZES[axis]
+    return lax.ppermute(block, axis, [(i, (i + step) % n) for i in range(n)])
+
+
+def scatter_sum_direct(rows, axes):
+    n = group_size(axes)
+    parts = lax.all_to_all(rows, axes, 0, 0, tiled=True)
+    return jnp.sum(parts.reshape((n, rows.shape[0] // n) + rows.shape[1:]), 0)
+
+
+def copies(block, axes):
+    n = group_size(axes)
+    sent = jnp.broadcast_to(block[None], (n,) + block.shape)
+    return lax.all_to_all(sent, axes, 0, 0, tiled=True)
+
+
+def gather_direct(block, axes):
+    return copies(block, axes).reshape((-1,) + block.shape[1:])
+
+
+def scatter_sum_ring(rows, axis):
+    n = SIZES[axis]
+    height = rows.shape[0] // n
+    me = lax.axis_index(axis)
+    arrived = [
+        shift(lax.dynamic_slice_in_dim(rows, lax.rem(me + k, n) * height, height, 0), axis, k)
+        for k in range(1, n)
+    ]
+    return lax.dynamic_slice_in_dim(rows, me * height, height, 0) + sum(arrived)
+
+
+def gather_ring(block, axis):
+    n = SIZES[axis]
+    height = block.shape[0]
+    me = lax.axis_index(axis)
+    out = jnp.zeros((height * n,) + block.shape[1:], block.dtype)
+    for k in range(n):
+        arrived = shift(block, axis, k) if k else block
+        out = lax.dynamic_update_slice_in_dim(out, arrived, lax.rem(me - k + n, n) * height, 0)
+    return out
+
+
+def sum_all(factor_part):
+    rows = factor_part.reshape(256, 128)
+    piece = scatter_sum_direct(rows, PLANE)
+    piece = jnp.sum(copies(piece, ("z",)), 0)
+    return gather_direct(piece, PLANE).reshape(factor_part.shape)
+
+
+def sum_dp(basis_term):
+    rows = basis_term.reshape(224, 1024)
+    piece = scatter_sum_ring(rows, "x")
+    piece = scatter_sum_direct(piece, ("z",))
+    piece = gather_direct(piece, ("z",))
+    return gather_ring(piece, "x").reshape(basis_term.shape)
 
 
 def cholesky_solve(gram_matrix, columns):
@@ -22,13 +88,12 @@
     factor_part = lax.dot_general(
         basis_low, corrected, (((1,), (1,)), ((), ())), preferred_element_type=jnp.float32
     )
-    factor_sum = lax.psum(factor_part, ("dp", "tensor"))
+    factor_sum = sum_all(factor_part)
     gram_matrix = jnp.dot(factor_sum, factor_sum.T, precision=lax.Precision.HIGHEST)
     factor_left = cholesky_solve(gram_matrix, factor_sum)
     factor_low = factor_left.astype(jnp.bfloat16)
-    replica_count = lax.axis_size("dp")
     basis_term = jnp.dot(factor_low, corrected, preferred_element_type=jnp.float32)
-    basis_next = lax.psum(basis_term, "dp") / replica_count
+    basis_next = sum_dp(basis_term) / (SIZES["z"] * SIZES["x"])
     basis_round = basis_next.astype(jnp.bfloat16)
     approx = lax.dot_general(
         factor_low, basis_round, (((0,), (0,)), ((), ())), preferred_element_type=jnp.float32
@@ -38,6 +103,8 @@
 
 
 def solution(mesh):
-    in_specs = (P("dp", None), P("dp", "tensor"), P("dp", "tensor"), P(None, "tensor"))
-    out_specs = (P(), P(None, "tensor"), P("dp", "tensor"))
-    return jax.shard_map(local, mesh=mesh, in_specs=in_specs, out_specs=out_specs, check_vma=False)
+    fine = Mesh(mesh.devices.reshape(8, 4, 4, 2), ("z", "x", "y", "c"))
+    dp, tensor = ("z", "x"), ("y", "c")
+    in_specs = (P(dp, None), P(dp, tensor), P(dp, tensor), P(None, tensor))
+    out_specs = (P(), P(None, tensor), P(dp, tensor))
+    return jax.shard_map(local, mesh=fine, in_specs=in_specs, out_specs=out_specs, check_vma=False)

time: 439 us -> 135 us (0.31)
  the two profiles are of different devices: /device:TPU:64 before, /device:TPU:6 now
where the time goes in v1:
time: 135 us; the launch traced here: 134 us
  blocking collectives  58.9 us (44%)
  waiting for transfers between devices  28.6 us (21%)
  matrix products  13.3 us (10%)
  other arithmetic  13.2 us (10%)
  starting transfers between devices  11.6 us (9%)
  local copies, waits for them, and re-layouts  8.04 us (6%)
    all_to_all x2, blocking collectives, copies(): return lax.all_to_all(sent, axes, 0, 0, tiled=True)  30.8 us
    all_to_all x2, blocking collectives, scatter_sum_direct(): parts = lax.all_to_all(rows, axes, 0, 0, tiled=True)  28.1 us
    ppermute x6, waiting for transfers between devices, shift(): return lax.ppermute(block, axis, [(i, (i + step) % n) for i in range(n)])  22.7 us
    another operation x3, other arithmetic, cholesky_solve(): lower_factor = jnp.linalg.cholesky(gram_matrix)  6.52 us
    all_to_all x1, waiting for transfers between devices, copies(): return lax.all_to_all(sent, axes, 0, 0, tiled=True)  5.86 us
    ppermute x6, starting transfers between devices, shift(): return lax.ppermute(block, axis, [(i, (i + step) % n) for i in range(n)])  5.82 us
    all_to_all x1, starting transfers between devices, copies(): return lax.all_to_all(sent, axes, 0, 0, tiled=True)  5.79 us
    another operation x2, other arithmetic, cholesky_solve(): return jax.scipy.linalg.solve_triangular(lower_factor, columns, lower=True)  5.55 us
  transfers between devices with their start and end apart: 7, of which 6 were waited for; matrix products, arithmetic and copies ran while one was open for 0% of the time, Pallas kernels for 0%

profile of v1, /device:TPU:6, one launch (start us, length us, event | category | flops | bytes accessed | tf_op | source)
XLA Modules:
  0.0 134.5 jit_solution(17082748804037451727)
XLA Ops:
  0.6 1.5 %copy-done = bf16[256,3584]{1,0:T(8,128)(2,1)S(1)} copy-done((bf16[256,3584]{1,0:T(8,128)(2,1)S(1)}, bf16[256,3584]{1,0:T(8,128)(2,1)}, u32[]{:S(2)}) %copy-start) | copy-done | bytes 1835032
  2.1 3.3 %add_convert_fusion = bf16[512,3584]{1,0:T(8,128)(2,1)S(1)} fusion(bf16[512,3584]{1,0:T(8,128)(2,1)} %param.6, bf16[256,512]{1,0:T(8,128)(2,1)} %param.4, bf16[256,3584]{1,0:T(8,128)(2,1)S(1)} %copy-done), kind=kOutput, calls=%fused_computation.1 | convolution fusion | flops 946864128 | bytes 9437184 | tf_op jit(solution)/shard_map/dot_general | solution.py:82
  5.5 1.8 %copy-done.1 = bf16[512,3584]{1,0:T(8,128)(2,1)} copy-done((bf16[512,3584]{1,0:T(8,128)(2,1)}, bf16[512,3584]{1,0:T(8,128)(2,1)S(1)}, u32[]{:S(2)}) %copy-start.1) | copy-done | bytes 3670040
  7.3 1.2 convolution_bitcast_fusion
  8.6 13.3 %all_to_all.33 = f32[32,8,128]{2,1,0:T(8,128)S(1)} all-to-all(f32[32,8,128]{2,1,0:T(8,128)S(1)} %all_to_all.21), channel_id=1, replica_groups=mesh['z'=8,'x'=4,'y'=4,'c'=2] {'x','y','c'}, dimensions={0} | all-to-all | bytes 262144 | tf_op jit(solution)/shard_map/all_to_all | solution.py:24
  21.9 16.3 %all_to_all.34 = f32[8,8,128]{2,1,0:T(8,128)S(1)} all-to-all(f32[8,8,128]{2,1,0:T(8,128)S(1)} %broadcast_in_dim.9), channel_id=1, replica_groups=mesh['z'=8,'x'=4,'y'=4,'c'=2] {'z'}, dimensions={0} | all-to-all | bytes 65536 | tf_op jit(solution)/shard_map/all_to_all | solution.py:31
  38.9 5.8 %all-to-all-start.2 = ((f32[32,8,128]{2,1,0:T(8,128)}), f32[32,8,128]{2,1,0:T(8,128)S(1)}, u32[]{:S(2)}, u32[]{:S(2)}) async-start(f32[32,8,128]{2,1,0:T(8,128)} %broadcast_in_dim.11), calls=%async_computation.2 | async-start | bytes 262144 | tf_op jit(solution)/shard_map/all_to_all | solution.py:31
  44.7 5.9 %all-to-all-done.2 = f32[32,8,128]{2,1,0:T(8,128)S(1)} async-done(((f32[32,8,128]{2,1,0:T(8,128)}), f32[32,8,128]{2,1,0:T(8,128)S(1)}, u32[]{:S(2)}, u32[]{:S(2)}) %all-to-all-start.2) | async-done | bytes 131104 | tf_op jit(solution)/shard_map/all_to_all | solution.py:31
  51.0 5.8 %cholesky.16 = f32[64,64]{1,0:T(8,128)S(1)} custom-call(f32[64,64]{1,0:T(8,128)S(1)} %fusion.5), custom_call_target="Cholesky" | custom-call | tf_op jit(solution)/shard_map/jit(cholesky)/cholesky | solution.py:76
  58.2 4.9 %custom-call.7 = f32[1,64,64]{1,2,0:T(8,128)S(1)} custom-call(f32[1,64,64]{2,1,0:T(8,128)S(1)} %fusion.2), custom_call_target="InvertDiagBlocksLowerTriangular" | custom-call | tf_op jit(solution)/shard_map/jit(_solve_triangular)/triangular_solve | solution.py:77
  63.4 2.8 %fusion.7 = f32[64,3584]{1,0:T(8,128)S(1)} fusion(bf16[512,3584]{1,0:T(8,128)(2,1)} %copy-done.1, f32[64,512]{1,0:T(8,128)S(1)} %fusion.3), kind=kOutput, calls=%fused_computation.14 | convolution fusion | flops 234913792 | bytes 4718592 | tf_op jit(solution)/shard_map/dot_general | solution.py:95
  66.3 1.2 reshape.38
  67.4 1.2 constant_dynamic-slice_fusion.1
  68.6 2.2 %collective-permute-start = (f32[56,1024]{1,0:T(8,128)S(1)}, f32[56,1024]{1,0:T(8,128)S(1)}, u32[]{:S(2)}, u32[]{:S(2)}) collective-permute-start(f32[56,1024]{1,0:T(8,128)S(1)} %get-tuple-element.5), channel_id=1, source_target_pairs={{0,8},{8,16},{16,24},{24,0},{1,9},{9,17},{17,25},{25,1},{2,10},{10... | collective-permute-start | bytes 688136 | tf_op jit(solution)/shard_map/ppermute | solution.py:19
  72.3 8.7 %collective-permute-done = f32[56,1024]{1,0:T(8,128)S(1)} collective-permute-done((f32[56,1024]{1,0:T(8,128)S(1)}, f32[56,1024]{1,0:T(8,128)S(1)}, u32[]{:S(2)}, u32[]{:S(2)}) %collective-permute-start) | collective-permute-done | bytes 229408 | tf_op jit(solution)/shard_map/ppermute | solution.py:19
  81.0 3.7 %collective-permute-done.2 = f32[56,1024]{1,0:T(8,128)S(1)} collective-permute-done((f32[56,1024]{1,0:T(8,128)S(1)}, f32[56,1024]{1,0:T(8,128)S(1)}, u32[]{:S(2)}, u32[]{:S(2)}) %collective-permute-start.2) | collective-permute-done | bytes 229408 | tf_op jit(solution)/shard_map/ppermute | solution.py:19
  85.7 14.7 %all_to_all.35 = f32[8,7,1024]{2,1,0:T(8,128)S(1)} all-to-all(f32[8,7,1024]{2,1,0:T(8,128)S(1)} %all_to_all.25), channel_id=1, replica_groups=mesh['z'=8,'x'=4,'y'=4,'c'=2] {'z'}, dimensions={0} | all-to-all | bytes 458752 | tf_op jit(solution)/shard_map/all_to_all | solution.py:24
  100.5 14.6 %all_to_all.36 = f32[8,7,1024]{2,1,0:T(8,128)S(1)} all-to-all(f32[8,7,1024]{2,1,0:T(8,128)S(1)} %broadcast_in_dim.13), channel_id=1, replica_groups=mesh['z'=8,'x'=4,'y'=4,'c'=2] {'z'}, dimensions={0} | all-to-all | bytes 458752 | tf_op jit(solution)/shard_map/all_to_all | solution.py:31
  115.9 1.3 collective-permute-start.5
  117.4 6.3 %collective-permute-done.3 = f32[56,1024]{1,0:T(8,128)S(1)} collective-permute-done((f32[56,1024]{1,0:T(8,128)S(1)}, f32[56,1024]{1,0:T(8,128)S(1)}, u32[]{:S(2)}, u32[]{:S(2)}) %collective-permute-start.3) | collective-permute-done | bytes 229408 | tf_op jit(solution)/shard_map/ppermute | solution.py:19
  123.7 1.6 %collective-permute-done.4 = f32[56,1024]{1,0:T(8,128)S(1)} collective-permute-done((f32[56,1024]{1,0:T(8,128)S(1)}, f32[56,1024]{1,0:T(8,128)S(1)}, u32[]{:S(2)}, u32[]{:S(2)}) %collective-permute-start.4) | collective-permute-done | bytes 229408 | tf_op jit(solution)/shard_map/ppermute | solution.py:19
  125.3 2.5 %collective-permute-done.5 = f32[56,1024]{1,0:T(8,128)S(1)} collective-permute-done((f32[56,1024]{1,0:T(8,128)S(1)}, f32[56,1024]{1,0:T(8,128)S(1)}, u32[]{:S(2)}, u32[]{:S(2)}) %collective-permute-start.5) | collective-permute-done | bytes 229408 | tf_op jit(solution)/shard_map/ppermute | solution.py:19
  127.9 1.3 div.20
  129.2 5.3 %subtract_convert_fusion = bf16[512,3584]{1,0:T(8,128)(2,1)} fusion(bf16[512,3584]{1,0:T(8,128)(2,1)} %copy-done.1, f32[64,3584]{1,0:T(8,128)} %div.20, f32[64,512]{1,0:T(8,128)S(1)} %fusion.3), kind=kOutput, calls=%fused_computation | convolution fusion | flops 240648192 | bytes 8388608 | tf_op jit(solution)/shard_map/dot_general | solution.py:98
  (35 shorter events, 6.4 us)
Async XLA Ops:
  0.6 1.5 %copy-start = (bf16[256,3584]{1,0:T(8,128)(2,1)S(1)}, bf16[256,3584]{1,0:T(8,128)(2,1)}, u32[]{:S(2)}) copy-start(bf16[256,3584]{1,0:T(8,128)(2,1)} %param.5) | copy-start | bytes 5505028
  2.1 5.2 %copy-start.3 = (f32[64,3584]{1,0:T(8,128)S(1)}, f32[64,3584]{1,0:T(8,128)}, u32[]{:S(2)}) copy-start(f32[64,3584]{1,0:T(8,128)} %param.7) | copy-start | bytes 2752516
  5.5 1.8 %copy-start.1 = (bf16[512,3584]{1,0:T(8,128)(2,1)}, bf16[512,3584]{1,0:T(8,128)(2,1)S(1)}, u32[]{:S(2)}) copy-start(bf16[512,3584]{1,0:T(8,128)(2,1)S(1)} %add_convert_fusion) | copy-start | bytes 11010052
  38.9 11.7 %all-to-all-start.2 = ((f32[32,8,128]{2,1,0:T(8,128)}), f32[32,8,128]{2,1,0:T(8,128)S(1)}, u32[]{:S(2)}, u32[]{:S(2)}) async-start(f32[32,8,128]{2,1,0:T(8,128)} %broadcast_in_dim.11), calls=%async_computation.2 | async-start | bytes 262144 | tf_op jit(solution)/shard_map/all_to_all | solution.py:31
  63.4 65.8 %copy-start.2 = (f32[64,512]{1,0:T(8,128)}, f32[64,512]{1,0:T(8,128)S(1)}, u32[]{:S(2)}) copy-start(f32[64,512]{1,0:T(8,128)S(1)} %fusion.3) | copy-start | bytes 393220
  68.6 12.3 %collective-permute-start = (f32[56,1024]{1,0:T(8,128)S(1)}, f32[56,1024]{1,0:T(8,128)S(1)}, u32[]{:S(2)}, u32[]{:S(2)}) collective-permute-start(f32[56,1024]{1,0:T(8,128)S(1)} %get-tuple-element.5), channel_id=1, source_target_pairs={{0,8},{8,16},{16,24},{24,0},{1,9},{9,17},{17,25},{25,1},{2,10},{10... | collective-permute-start | bytes 688136 | tf_op jit(solution)/shard_map/ppermute | solution.py:19
  70.9 10.1 %collective-permute-start.1 = (f32[56,1024]{1,0:T(8,128)S(1)}, f32[56,1024]{1,0:T(8,128)S(1)}, u32[]{:S(2)}, u32[]{:S(2)}) collective-permute-start(f32[56,1024]{1,0:T(8,128)S(1)} %get-tuple-element.3), channel_id=1, source_target_pairs={{0,16},{8,24},{16,0},{24,8},{1,17},{9,25},{17,1},{25,9},{2,18},{10... | collective-permute-start | bytes 688136 | tf_op jit(solution)/shard_map/ppermute | solution.py:19
  71.5 13.1 %collective-permute-start.2 = (f32[56,1024]{1,0:T(8,128)S(1)}, f32[56,1024]{1,0:T(8,128)S(1)}, u32[]{:S(2)}, u32[]{:S(2)}) collective-permute-start(f32[56,1024]{1,0:T(8,128)S(1)} %get-tuple-element.4), channel_id=1, source_target_pairs={{0,24},{8,0},{16,8},{24,16},{1,25},{9,1},{17,9},{25,17},{2,26},{10... | collective-permute-start | bytes 688136 | tf_op jit(solution)/shard_map/ppermute | solution.py:19
  115.1 8.6 %collective-permute-start.3 = (f32[56,1024]{1,0:T(8,128)S(1)}, f32[56,1024]{1,0:T(8,128)S(1)}, u32[]{:S(2)}, u32[]{:S(2)}) collective-permute-start(f32[56,1024]{1,0:T(8,128)S(1)} %reshape.39), channel_id=1, source_target_pairs={{0,8},{8,16},{16,24},{24,0},{1,9},{9,17},{17,25},{25,1},{2,10},{10... | collective-permute-start | bytes 688136 | tf_op jit(solution)/shard_map/ppermute | solution.py:19
  115.2 10.2 %collective-permute-start.4 = (f32[56,1024]{1,0:T(8,128)S(1)}, f32[56,1024]{1,0:T(8,128)S(1)}, u32[]{:S(2)}, u32[]{:S(2)}) collective-permute-start(f32[56,1024]{1,0:T(8,128)S(1)} %reshape.39), channel_id=1, source_target_pairs={{0,16},{8,24},{16,0},{24,8},{1,17},{9,25},{17,1},{25,9},{2,18},{10... | collective-permute-start | bytes 688136 | tf_op jit(solution)/shard_map/ppermute | solution.py:19
  115.9 11.9 %collective-permute-start.5 = (f32[56,1024]{1,0:T(8,128)S(1)}, f32[56,1024]{1,0:T(8,128)S(1)}, u32[]{:S(2)}, u32[]{:S(2)}) collective-permute-start(f32[56,1024]{1,0:T(8,128)S(1)} %reshape.39), channel_id=1, source_target_pairs={{0,24},{8,0},{16,8},{24,16},{1,25},{9,1},{17,9},{25,17},{2,26},{10... | collective-permute-start | bytes 688136 | tf_op jit(solution)/shard_map/ppermute | solution.py:19

commit v2 on v0

v2 whole, which is shorter than its diff:
```python
import functools
import math

import jax
import jax.numpy as jnp
from jax import lax
from jax.experimental import pallas as pl
from jax.experimental.pallas import tpu as pltpu
from jax.sharding import Mesh
from jax.sharding import PartitionSpec as P

SIZES = dict(z=8, x=4, y=4, c=2)
PLANE = ("x", "y", "c")
REPLICAS = SIZES["z"] * SIZES["x"]
QUARTERS = SIZES["x"]
VMEM = pltpu.CompilerParams(vmem_limit_bytes=32 << 20)


def shift(block, axis, step):
    n = SIZES[axis]
    return lax.ppermute(block, axis, [(i, (i + step) % n) for i in range(n)])


def copies(block, axes):
    n = math.prod(SIZES[a] for a in axes)
    sent = jnp.broadcast_to(block[None], (n,) + block.shape)
    return lax.all_to_all(sent, axes, 0, 0, tiled=True)


def sum_all(tiles):
    piece = jnp.sum(lax.all_to_all(tiles, PLANE, 0, 0, tiled=True), 0)
    piece = jnp.sum(copies(piece, ("z",)), 0)
    return copies(piece, PLANE)


def corrected_kernel(x_ref, g_ref, fb_ref, basis_ref, corrected_ref, tiles_ref, xt_ref, acc_ref):
    step = pl.program_id(0)

    @pl.when(step == 0)
    def _():
        xt_ref[...] = x_ref[...].T
        acc_ref[...] = jnp.zeros_like(acc_ref)

    grad = jnp.dot(xt_ref[...], g_ref[...], preferred_element_type=jnp.float32)
    grad = grad * (1.0 / math.sqrt(x_ref.shape[0])) + fb_ref[...].astype(jnp.float32)
    corrected = grad.astype(jnp.bfloat16)
    corrected_ref[0] = corrected
    acc_ref[...] += lax.dot_general(
        basis_ref[...].astype(jnp.bfloat16),
        corrected,
        (((1,), (1,)), ((), ())),
        preferred_element_type=jnp.float32,
    )

    @pl.when(step == pl.num_programs(0) - 1)
    def _():
        rows, columns = acc_ref.shape
        for i in range(rows // 8):
            for j in range(columns // 128):
                tiles_ref[i * (columns // 128) + j] = acc_ref[8 * i : 8 * i + 8, 128 * j : 128 * j + 128]


def corrected_and_factor(layer_input, output_grad, feedback, basis_prev):
    tokens, rows = layer_input.shape
    columns, rank = output_grad.shape[1], basis_prev.shape[0]
    width = columns // QUARTERS
    return pl.pallas_call(
        corrected_kernel,
        grid=(QUARTERS,),
        in_specs=[
            pl.BlockSpec((tokens, rows), lambda q: (0, 0)),
            pl.BlockSpec((tokens, width), lambda q: (0, q)),
            pl.BlockSpec((rows, width), lambda q: (0, q)),
            pl.BlockSpec((rank, width), lambda q: (0, q)),
        ],
        out_specs=[
            pl.BlockSpec((1, rows, width), lambda q: (q, 0, 0)),
            pl.BlockSpec((rank * rows // 1024, 8, 128), lambda q: (0, 0, 0)),
        ],
        out_shape=[
            jax.ShapeDtypeStruct((QUARTERS, rows, width), jnp.bfloat16),
            jax.ShapeDtypeStruct((rank * rows // 1024, 8, 128), jnp.float32),
        ],
        scratch_shapes=[
            pltpu.VMEM((rows, tokens), jnp.bfloat16),
            pltpu.VMEM((rank, rows), jnp.float32),
        ],
        compiler_params=VMEM,
        name="corrected",
    )(layer_input, output_grad, feedback, basis_prev)


def eliminate(factor):
    rank, columns = factor.shape
    both = jnp.concatenate([factor, factor], 0)
    gram = lax.dot_general(
        factor,
        both,
        (((1,), (1,)), ((), ())),
        preferred_element_type=jnp.float32,
        precision=lax.Precision.HIGHEST,
    )
    blocks = rank // 8
    lanes = columns // 128
    table = [
        [gram[8 * i : 8 * i + 8]]
        + [factor[8 * i : 8 * i + 8, 128 * j : 128 * j + 128] for j in range(lanes)]
        for i in range(blocks)
    ]
    sublane = lax.broadcasted_iota(jnp.int32, (8, 128), 0)
    spread = lambda row: jnp.broadcast_to(row, (8, 128))
    out = []
    for p in range(blocks):
        below = range(p, blocks)
        col = [
            {i: jnp.broadcast_to(table[i][0][:, 8 * p + j : 8 * p + j + 1], (8, 128)) for i in below}
            for j in range(8)
        ]
        pivots = jnp.ones((8, 128), jnp.float32)
        for j in range(8):
            pivot = spread(col[j][p][j : j + 1])
            pivots = jnp.where(sublane == j, pivot, pivots)
            if p == blocks - 1 and j == 7:
                break
            inverse = 1.0 / pivot
            mult = {i: col[j][i] * inverse for i in below}
            mult[p] = jnp.where(sublane > j, mult[p], 0.0)
            for k in range(j + 1, 8):
                entry = spread(col[j][p][k : k + 1])
                for i in below:
                    col[k][i] = col[k][i] - mult[i] * entry
            for t in range(lanes + 1):
                if t == 0 and p == blocks - 1:
                    continue
                row = spread(table[p][t][j : j + 1])
                for i in below:
                    table[i][t] = table[i][t] - mult[i] * row
        scale = lax.rsqrt(pivots)
        out.append([table[p][t] * scale for t in range(1, lanes + 1)])
    return out


def factor_kernel(me_ref, tiles_ref, corrected_hbm, left_ref, low_ref, *rest):
    term_refs, (corrected_ref, sem) = rest[:QUARTERS], rest[QUARTERS:]
    copy = pltpu.make_async_copy(corrected_hbm, corrected_ref, sem)
    copy.start()
    rank, columns = left_ref.shape
    lanes = columns // 128
    factor = jnp.concatenate(
        [
            jnp.concatenate([tiles_ref[i * lanes + j] for j in range(lanes)], 1)
            for i in range(rank // 8)
        ],
        0,
    )
    blocks = eliminate(factor)
    for i, block in enumerate(blocks):
        for j, tile in enumerate(block):
            left_ref[8 * i : 8 * i + 8, 128 * j : 128 * j + 128] = tile
    low = left_ref[...].astype(jnp.bfloat16)
    low_ref[...] = low
    copy.wait()
    me = me_ref[0]
    for k in range(QUARTERS):
        quarter = lax.rem(me + k, QUARTERS)
        term_refs[k][...] = jnp.dot(low, corrected_ref[quarter], preferred_element_type=jnp.float32)


def factor_and_terms(me, tiles, corrected, rank):
    quarters, rows, width = corrected.shape
    whole = pl.BlockSpec(memory_space=pltpu.VMEM)
    return pl.pallas_call(
        factor_kernel,
        in_specs=[
            pl.BlockSpec(memory_space=pltpu.SMEM),
            whole,
            pl.BlockSpec(memory_space=pl.ANY),
        ],
        out_specs=[whole] * (2 + quarters),
        out_shape=[
            jax.ShapeDtypeStruct((rank, rows), jnp.float32),
            jax.ShapeDtypeStruct((rank, rows), jnp.bfloat16),
        ]
        + [jax.ShapeDtypeStruct((rank, width), jnp.float32)] * quarters,
        scratch_shapes=[pltpu.VMEM(corrected.shape, jnp.bfloat16), pltpu.SemaphoreType.DMA(())],
        compiler_params=VMEM,
        name="factor",
    )(me, tiles, corrected)


def feedback_kernel(q_ref, total_ref, low_t_ref, corrected_ref, *rest):
    next_ref, feedback_ref = rest[-2:]
    basis_next = total_ref[...] * (1.0 / REPLICAS)
    next_ref[...] = basis_next
    approx = jnp.dot(
        low_t_ref[...], basis_next.astype(jnp.bfloat16), preferred_element_type=jnp.float32
    )
    feedback_ref[...] = (corrected_ref[0].astype(jnp.float32) - approx).astype(jnp.bfloat16)


def finish_quarter(quarter, total, low_t, corrected, so_far):
    quarters, rows, width = corrected.shape
    rank = total.shape[0]
    return pl.pallas_call(
        feedback_kernel,
        grid_spec=pltpu.PrefetchScalarGridSpec(
            num_scalar_prefetch=1,
            grid=(1,),
            in_specs=[
                pl.BlockSpec((rank, width), lambda s, q: (0, 0)),
                pl.BlockSpec((rows, rank), lambda s, q: (0, 0)),
                pl.BlockSpec((1, rows, width), lambda s, q: (q[0], 0, 0)),
            ]
            + [pl.BlockSpec(memory_space=pl.ANY)] * len(so_far),
            out_specs=[
                pl.BlockSpec((rank, width), lambda s, q: (0, q[0])),
                pl.BlockSpec((rows, width), lambda s, q: (0, q[0])),
            ],
        ),
        out_shape=[
            jax.ShapeDtypeStruct((rank, width * quarters), jnp.float32),
            jax.ShapeDtypeStruct((rows, width * quarters), jnp.bfloat16),
        ],
        input_output_aliases={4: 0, 5: 1} if so_far else {},
        compiler_params=VMEM,
        name="feedback",
    )(quarter, total, low_t, corrected, *so_far)


def local(layer_input, output_grad, feedback, basis_prev):
    me = lax.axis_index("x").reshape(1)
    corrected, tiles = corrected_and_factor(layer_input, output_grad, feedback, basis_prev)
    tiles = sum_all(tiles)
    factor_left, factor_low, *terms = factor_and_terms(me, tiles, corrected, basis_prev.shape[0])
    factor_low_t = factor_low.T

    arrived = [shift(terms[k], "x", k) for k in range(1, QUARTERS)]
    quarter = terms[0] + sum(arrived)
    piece = lax.all_to_all(quarter.reshape(SIZES["z"], 8, -1), "z", 0, 0, tiled=True)
    piece = jnp.sum(piece, 0)
    quarter = copies(piece, ("z",)).reshape(quarter.shape)
    totals = [quarter] + [shift(quarter, "x", k) for k in range(1, QUARTERS)]
    results = ()
    for k in range(QUARTERS):
        owner = lax.rem(me + (QUARTERS - k), QUARTERS)
        results = finish_quarter(owner, totals[k], factor_low_t, corrected, results)
    return (factor_left,) + tuple(results)


def solution(mesh):
    fine = Mesh(mesh.devices.reshape(8, 4, 4, 2), ("z", "x", "y", "c"))
    dp, tensor = ("z", "x"), ("y", "c")
    in_specs = (P(dp, None), P(dp, tensor), P(dp, tensor), P(None, tensor))
    out_specs = (P(), P(None, tensor), P(dp, tensor))
    return jax.shard_map(local, mesh=fine, in_specs=in_specs, out_specs=out_specs, check_vma=False)
```

time: 439 us -> 117 us (0.27)
  the two profiles are of different devices: /device:TPU:64 before, /device:TPU:8 now
where the time goes in v2:
time: 117 us
  blocking collectives  55.7 us (48%)
  waiting for transfers between devices  20.5 us (18%)
  starting transfers between devices  15.1 us (13%)
  local copies, waits for them, and re-layouts  12.4 us (11%)
  Pallas kernels  12.3 us (11%)
    all_to_all x2, blocking collectives, copies(): return lax.all_to_all(sent, axes, 0, 0, tiled=True)  28.8 us
    all_to_all x1, blocking collectives, sum_all(): piece = jnp.sum(lax.all_to_all(tiles, PLANE, 0, 0, tiled=True), 0)  13.9 us
    ppermute x6, waiting for transfers between devices, shift(): return lax.ppermute(block, axis, [(i, (i + step) % n) for i in range(n)])  13.8 us
    all_to_all x1, blocking collectives, local(): lax.all_to_all(quarter.reshape(SIZES['z'], 8, -1), 'z', 0, 0, tiled=True)  13 us
    unnamed x14, local copies, waits for them, and re-layouts  11.6 us
    ppermute x6, starting transfers between devices, shift(): return lax.ppermute(block, axis, [(i, (i + step) % n) for i in range(n)])  10.1 us
    all_to_all x1, waiting for transfers between devices, copies(): return lax.all_to_all(sent, axes, 0, 0, tiled=True)  6.71 us
    pallas_call x4, Pallas kernels, finish_quarter(): pl.pallas_call(feedback_kernel, grid_spec=pltpu.PrefetchScalarGridSpec(nu...  5.23 us
  transfers between devices with their start and end apart: 7, of which 5 were waited for; matrix products, arithmetic and copies ran while one was open for 0% of the time, Pallas kernels for 3%

profile of v2, /device:TPU:8, one launch (start us, length us, event | category | flops | bytes accessed | tf_op | source)
XLA Modules:
  0.0 116.8 jit_solution(6833238809104028418)
XLA Ops:
  0.6 2.0 %copy-done.3 = bf16[512,3584]{1,0:T(8,128)(2,1)S(1)} copy-done((bf16[512,3584]{1,0:T(8,128)(2,1)S(1)}, bf16[512,3584]{1,0:T(8,128)(2,1)}, u32[]{:S(2)}) %copy-start.3) | copy-done | bytes 3670040
  2.7 1.5 %copy-done.4 = bf16[256,3584]{1,0:T(8,128)(2,1)S(1)} copy-done((bf16[256,3584]{1,0:T(8,128)(2,1)S(1)}, bf16[256,3584]{1,0:T(8,128)(2,1)}, u32[]{:S(2)}) %copy-start.4) | copy-done | bytes 1835032
  6.3 3.3 %corrected.1 = (bf16[4,512,896]{2,1,0:T(8,128)(2,1)S(1)}, f32[32,8,128]{2,1,0:T(8,128)S(1)}) custom-call(bf16[256,512]{1,0:T(8,128)(2,1)S(1)} %copy-done.6, bf16[256,3584]{1,0:T(8,128)(2,1)S(1)} %copy-done.4, bf16[512,3584]{1,0:T(8,128)(2,1)S(1)} %copy-done.3, f32[64,3584]{1,0:T(8,128)S(1)} %copy-done.5), custom_call_target="tpu_custom_call" | custom-call | tf_op jit(solution)/shard_map/corrected/pallas_call | solution.py:67
  9.6 1.8 %copy-done = bf16[4,512,896]{2,1,0:T(8,128)(2,1)} copy-done((bf16[4,512,896]{2,1,0:T(8,128)(2,1)}, bf16[4,512,896]{2,1,0:T(8,128)(2,1)S(1)}, u32[]{:S(2)}) %copy-start) | copy-done | bytes 3670040
  11.5 13.9 %all_to_all.25 = f32[32,8,128]{2,1,0:T(8,128)S(1)} all-to-all(f32[32,8,128]{2,1,0:T(8,128)S(1)} %get-tuple-element.19), channel_id=1, replica_groups=mesh['z'=8,'x'=4,'y'=4,'c'=2] {'x','y','c'}, dimensions={0} | all-to-all | bytes 262144 | tf_op jit(solution)/shard_map/all_to_all | solution.py:31
  25.4 16.3 %all_to_all.26 = f32[8,8,128]{2,1,0:T(8,128)S(1)} all-to-all(f32[8,8,128]{2,1,0:T(8,128)S(1)} %broadcast_in_dim.6), channel_id=1, replica_groups=mesh['z'=8,'x'=4,'y'=4,'c'=2] {'z'}, dimensions={0} | all-to-all | bytes 65536 | tf_op jit(solution)/shard_map/all_to_all | solution.py:27
  42.4 5.0 %all-to-all-start.2 = ((f32[32,8,128]{2,1,0:T(8,128)}), f32[32,8,128]{2,1,0:T(8,128)S(1)}, u32[]{:S(2)}, u32[]{:S(2)}) async-start(f32[32,8,128]{2,1,0:T(8,128)} %broadcast_in_dim.7), calls=%async_computation.2 | async-start | bytes 262144 | tf_op jit(solution)/shard_map/all_to_all | solution.py:27
  47.4 6.7 %all-to-all-done.2.tiles_ref = f32[32,8,128]{2,1,0:T(8,128)S(1)} async-done(((f32[32,8,128]{2,1,0:T(8,128)}), f32[32,8,128]{2,1,0:T(8,128)S(1)}, u32[]{:S(2)}, u32[]{:S(2)}) %all-to-all-start.2) | async-done | bytes 131104 | tf_op jit(solution)/shard_map/all_to_all | solution.py:27
  54.1 2.0 %copy-done.1 = bf16[4,512,896]{2,1,0:T(8,128)(2,1)S(1)} copy-done((bf16[4,512,896]{2,1,0:T(8,128)(2,1)S(1)}, bf16[4,512,896]{2,1,0:T(8,128)(2,1)}, u32[]{:S(2)}) %copy-start.1) | copy-done | bytes 3670040
  56.2 3.7 %factor.1 = (f32[64,512]{1,0:T(8,128)}, bf16[64,512]{1,0:T(8,128)(2,1)S(1)}, f32[64,896]{1,0:T(8,128)S(1)}, f32[64,896]{1,0:T(8,128)S(1)}, f32[64,896]{1,0:T(8,128)S(1)}, /*index=5*/f32[64,896]{1,0:T(8,128)S(1)}) custom-call(s32[1]{0:T(128)} %bitcast.me_ref, f32[32,8,128]{2,1,0:T(8,128)S(1)} %all-to-all-done.2.tiles_ref, bf16[4,512,896]{2,1,0:T(8,128)(2,1)S(1)} %copy-done.1), custom_call_target="tpu_custom_call" | custom-call | tf_op jit(solution)/shard_map/factor/pallas_call | solution.py:172
  60.6 2.0 %collective-permute-start.1 = (f32[64,896]{1,0:T(8,128)S(1)}, f32[64,896]{1,0:T(8,128)S(1)}, u32[]{:S(2)}, u32[]{:S(2)}) collective-permute-start(f32[64,896]{1,0:T(8,128)S(1)} %get-tuple-element.24), channel_id=1, source_target_pairs={{0,16},{8,24},{16,0},{24,8},{1,17},{9,25},{17,1},{25,9},{2,18},{10... | collective-permute-start | bytes 688136 | tf_op jit(solution)/shard_map/ppermute | solution.py:21
  62.6 1.4 %collective-permute-start.2 = (f32[64,896]{1,0:T(8,128)S(1)}, f32[64,896]{1,0:T(8,128)S(1)}, u32[]{:S(2)}, u32[]{:S(2)}) collective-permute-start(f32[64,896]{1,0:T(8,128)S(1)} %get-tuple-element.25), channel_id=1, source_target_pairs={{0,24},{8,0},{16,8},{24,16},{1,25},{9,1},{17,9},{25,17},{2,26},{10... | collective-permute-start | bytes 688136 | tf_op jit(solution)/shard_map/ppermute | solution.py:21
  63.9 9.8 %collective-permute-done = f32[64,896]{1,0:T(8,128)S(1)} collective-permute-done((f32[64,896]{1,0:T(8,128)S(1)}, f32[64,896]{1,0:T(8,128)S(1)}, u32[]{:S(2)}, u32[]{:S(2)}) %collective-permute-start) | collective-permute-done | bytes 229408 | tf_op jit(solution)/shard_map/ppermute | solution.py:21
  74.4 13.0 %all_to_all.27 = f32[8,8,896]{2,1,0:T(8,128)S(1)} all-to-all(f32[8,8,896]{2,1,0:T(8,128)S(1)} %add_bitcast_fusion), channel_id=1, replica_groups=mesh['z'=8,'x'=4,'y'=4,'c'=2] {'z'}, dimensions={0} | all-to-all | bytes 458752 | tf_op jit(solution)/shard_map/all_to_all | solution.py:239
  87.4 12.5 %all_to_all.28 = f32[8,8,896]{2,1,0:T(8,128)S(1)} all-to-all(f32[8,8,896]{2,1,0:T(8,128)S(1)} %broadcast_in_dim.8), channel_id=1, replica_groups=mesh['z'=8,'x'=4,'y'=4,'c'=2] {'z'}, dimensions={0} | all-to-all | bytes 458752 | tf_op jit(solution)/shard_map/all_to_all | solution.py:27
  100.0 2.7 %collective-permute-start.5 = (f32[64,896]{1,0:T(8,128)S(1)}, f32[64,896]{1,0:T(8,128)S(1)}, u32[]{:S(2)}, u32[]{:S(2)}) collective-permute-start(f32[64,896]{1,0:T(8,128)S(1)} %bitcast.9), channel_id=1, source_target_pairs={{0,8},{8,16},{16,24},{24,0},{1,9},{9,17},{17,25},{25,1},{2,10},{10... | collective-permute-start | bytes 688136 | tf_op jit(solution)/shard_map/ppermute | solution.py:21
  102.6 3.4 %collective-permute-start.4 = (f32[64,896]{1,0:T(8,128)S(1)}, f32[64,896]{1,0:T(8,128)S(1)}, u32[]{:S(2)}, u32[]{:S(2)}) collective-permute-start(f32[64,896]{1,0:T(8,128)S(1)} %bitcast.10), channel_id=1, source_target_pairs={{0,16},{8,24},{16,0},{24,8},{1,17},{9,25},{17,1},{25,9},{2,18},{10... | collective-permute-start | bytes 688136 | tf_op jit(solution)/shard_map/ppermute | solution.py:21
  106.2 2.0 %copy-done.2 = bf16[4,512,896]{2,1,0:T(8,128)(2,1)S(1)} copy-done((bf16[4,512,896]{2,1,0:T(8,128)(2,1)S(1)}, bf16[4,512,896]{2,1,0:T(8,128)(2,1)}, u32[]{:S(2)}) %copy-start.2) | copy-done | bytes 3670040
  108.2 1.3 %feedback.4 = (f32[64,3584]{1,0:T(8,128)}, bf16[512,3584]{1,0:T(8,128)(2,1)}) custom-call(s32[1]{0:T(128)S(6)} %rem.75.q_ref, f32[64,896]{1,0:T(8,128)S(1)} %bitcast.12, bf16[512,64]{1,0:T(8,128)(2,1)S(1)} %bitcast.5, bf16[4,512,896]{2,1,0:T(8,128)(2,1)S(1)} %copy-done.2), custom_call_target="tpu_custom_call" | custom-call | tf_op jit(solution)/shard_map/feedback/pallas_call | solution.py:204
  109.5 1.5 %collective-permute-done.5.total_ref = f32[64,896]{1,0:T(8,128)S(1)} collective-permute-done((f32[64,896]{1,0:T(8,128)S(1)}, f32[64,896]{1,0:T(8,128)S(1)}, u32[]{:S(2)}, u32[]{:S(2)}) %collective-permute-start.5) | collective-permute-done | bytes 229408 | tf_op jit(solution)/shard_map/ppermute | solution.py:21
  111.0 1.3 %feedback.5 = (f32[64,3584]{1,0:T(8,128)}, bf16[512,3584]{1,0:T(8,128)(2,1)}) custom-call(s32[1]{0:T(128)S(6)} %rem.69.q_ref, f32[64,896]{1,0:T(8,128)S(1)} %collective-permute-done.5.total_ref, bf16[512,64]{1,0:T(8,128)(2,1)S(1)} %bitcast.6, bf16[4,512,896]{2,1,0:T(8,128)(2,1)S(1)} %copy-done.2, ...), custom_call_target="tpu_custom_call", output_to_operand_aliasing={{0}: (4, {}), {1}: (5, {})} | custom-call | tf_op jit(solution)/shard_map/feedback/pallas_call | solution.py:204
  112.4 1.8 %collective-permute-done.4.total_ref = f32[64,896]{1,0:T(8,128)S(1)} collective-permute-done((f32[64,896]{1,0:T(8,128)S(1)}, f32[64,896]{1,0:T(8,128)S(1)}, u32[]{:S(2)}, u32[]{:S(2)}) %collective-permute-start.4) | collective-permute-done | bytes 229408 | tf_op jit(solution)/shard_map/ppermute | solution.py:21
  114.2 1.3 %feedback.6 = (f32[64,3584]{1,0:T(8,128)}, bf16[512,3584]{1,0:T(8,128)(2,1)}) custom-call(s32[1]{0:T(128)S(6)} %rem.63.q_ref, f32[64,896]{1,0:T(8,128)S(1)} %collective-permute-done.4.total_ref, bf16[512,64]{1,0:T(8,128)(2,1)S(1)} %bitcast.7, bf16[4,512,896]{2,1,0:T(8,128)(2,1)S(1)} %copy-done.2, ...), custom_call_target="tpu_custom_call", output_to_operand_aliasing={{0}: (4, {}), {1}: (5, {})} | custom-call | tf_op jit(solution)/shard_map/feedback/pallas_call | solution.py:204
  115.5 1.3 %feedback.7 = (f32[64,3584]{1,0:T(8,128)}, bf16[512,3584]{1,0:T(8,128)(2,1)}) custom-call(s32[1]{0:T(128)S(6)} %rem.57.q_ref, f32[64,896]{1,0:T(8,128)S(1)} %collective-permute-done.3.total_ref, bf16[512,64]{1,0:T(8,128)(2,1)S(1)} %bitcast.8, bf16[4,512,896]{2,1,0:T(8,128)(2,1)S(1)} %copy-done.2, ...), custom_call_target="tpu_custom_call", output_to_operand_aliasing={{0}: (4, {}), {1}: (5, {})} | custom-call | tf_op jit(solution)/shard_map/feedback/pallas_call | solution.py:204
  (22 shorter events, 4.4 us)
Async XLA Ops:
  0.6 2.0 %copy-start.3 = (bf16[512,3584]{1,0:T(8,128)(2,1)S(1)}, bf16[512,3584]{1,0:T(8,128)(2,1)}, u32[]{:S(2)}) copy-start(bf16[512,3584]{1,0:T(8,128)(2,1)} %fb_ref.1) | copy-start | bytes 11010052
  2.7 1.5 %copy-start.4 = (bf16[256,3584]{1,0:T(8,128)(2,1)S(1)}, bf16[256,3584]{1,0:T(8,128)(2,1)}, u32[]{:S(2)}) copy-start(bf16[256,3584]{1,0:T(8,128)(2,1)} %g_ref.1) | copy-start | bytes 5505028
  4.2 1.2 %copy-start.5 = (f32[64,3584]{1,0:T(8,128)S(1)}, f32[64,3584]{1,0:T(8,128)}, u32[]{:S(2)}) copy-start(f32[64,3584]{1,0:T(8,128)} %basis_ref.1) | copy-start | bytes 2752516
  5.3 0.9 copy-start.6
  9.6 1.8 %copy-start = (bf16[4,512,896]{2,1,0:T(8,128)(2,1)}, bf16[4,512,896]{2,1,0:T(8,128)(2,1)S(1)}, u32[]{:S(2)}) copy-start(bf16[4,512,896]{2,1,0:T(8,128)(2,1)S(1)} %get-tuple-element.20.corrected_hbm.corrected_ref) | copy-start | bytes 11010052
  42.4 11.7 %all-to-all-start.2 = ((f32[32,8,128]{2,1,0:T(8,128)}), f32[32,8,128]{2,1,0:T(8,128)S(1)}, u32[]{:S(2)}, u32[]{:S(2)}) async-start(f32[32,8,128]{2,1,0:T(8,128)} %broadcast_in_dim.7), calls=%async_computation.2 | async-start | bytes 262144 | tf_op jit(solution)/shard_map/all_to_all | solution.py:27
  54.1 2.0 %copy-start.1 = (bf16[4,512,896]{2,1,0:T(8,128)(2,1)S(1)}, bf16[4,512,896]{2,1,0:T(8,128)(2,1)}, u32[]{:S(2)}) copy-start(bf16[4,512,896]{2,1,0:T(8,128)(2,1)} %copy-done) | copy-start | bytes 11010052
  59.9 13.8 %collective-permute-start = (f32[64,896]{1,0:T(8,128)S(1)}, f32[64,896]{1,0:T(8,128)S(1)}, u32[]{:S(2)}, u32[]{:S(2)}) collective-permute-start(f32[64,896]{1,0:T(8,128)S(1)} %get-tuple-element.23), channel_id=1, source_target_pairs={{0,8},{8,16},{16,24},{24,0},{1,9},{9,17},{17,25},{25,1},{2,10},{10... | collective-permute-start | bytes 688136 | tf_op jit(solution)/shard_map/ppermute | solution.py:21
  60.6 13.1 %collective-permute-start.1 = (f32[64,896]{1,0:T(8,128)S(1)}, f32[64,896]{1,0:T(8,128)S(1)}, u32[]{:S(2)}, u32[]{:S(2)}) collective-permute-start(f32[64,896]{1,0:T(8,128)S(1)} %get-tuple-element.24), channel_id=1, source_target_pairs={{0,16},{8,24},{16,0},{24,8},{1,17},{9,25},{17,1},{25,9},{2,18},{10... | collective-permute-start | bytes 688136 | tf_op jit(solution)/shard_map/ppermute | solution.py:21
  62.6 11.8 %collective-permute-start.2 = (f32[64,896]{1,0:T(8,128)S(1)}, f32[64,896]{1,0:T(8,128)S(1)}, u32[]{:S(2)}, u32[]{:S(2)}) collective-permute-start(f32[64,896]{1,0:T(8,128)S(1)} %get-tuple-element.25), channel_id=1, source_target_pairs={{0,24},{8,0},{16,8},{24,16},{1,25},{9,1},{17,9},{25,17},{2,26},{10... | collective-permute-start | bytes 688136 | tf_op jit(solution)/shard_map/ppermute | solution.py:21
  100.0 11.1 %collective-permute-start.5 = (f32[64,896]{1,0:T(8,128)S(1)}, f32[64,896]{1,0:T(8,128)S(1)}, u32[]{:S(2)}, u32[]{:S(2)}) collective-permute-start(f32[64,896]{1,0:T(8,128)S(1)} %bitcast.9), channel_id=1, source_target_pairs={{0,8},{8,16},{16,24},{24,0},{1,9},{9,17},{17,25},{25,1},{2,10},{10... | collective-permute-start | bytes 688136 | tf_op jit(solution)/shard_map/ppermute | solution.py:21
  102.6 11.6 %collective-permute-start.4 = (f32[64,896]{1,0:T(8,128)S(1)}, f32[64,896]{1,0:T(8,128)S(1)}, u32[]{:S(2)}, u32[]{:S(2)}) collective-permute-start(f32[64,896]{1,0:T(8,128)S(1)} %bitcast.10), channel_id=1, source_target_pairs={{0,16},{8,24},{16,0},{24,8},{1,17},{9,25},{17,1},{25,9},{2,18},{10... | collective-permute-start | bytes 688136 | tf_op jit(solution)/shard_map/ppermute | solution.py:21
  106.0 9.5 %collective-permute-start.3 = (f32[64,896]{1,0:T(8,128)S(1)}, f32[64,896]{1,0:T(8,128)S(1)}, u32[]{:S(2)}, u32[]{:S(2)}) collective-permute-start(f32[64,896]{1,0:T(8,128)S(1)} %bitcast.11), channel_id=1, source_target_pairs={{0,24},{8,0},{16,8},{24,16},{1,25},{9,1},{17,9},{25,17},{2,26},{10... | collective-permute-start | bytes 688136 | tf_op jit(solution)/shard_map/ppermute | solution.py:21
  106.2 2.0 %copy-start.2 = (bf16[4,512,896]{2,1,0:T(8,128)(2,1)S(1)}, bf16[4,512,896]{2,1,0:T(8,128)(2,1)}, u32[]{:S(2)}) copy-start(bf16[4,512,896]{2,1,0:T(8,128)(2,1)} %copy-done) | copy-start | bytes 11010052

commit v3 on v2

v3 whole, which is shorter than its diff:
```python
import functools
import math

import jax
import jax.numpy as jnp
from jax import lax
from jax.experimental import pallas as pl
from jax.experimental.pallas import tpu as pltpu
from jax.sharding import Mesh
from jax.sharding import PartitionSpec as P

SIZES = dict(z=8, x=4, y=4, c=2)
PLANE = ("x", "y", "c")
REPLICAS = SIZES["z"] * SIZES["x"]
QUARTERS = SIZES["x"]
STRIPS = 4
ARRIVING = (0, 1, 3, 2)
VMEM = pltpu.CompilerParams(vmem_limit_bytes=24 << 20)


def in_hbm(*arrays):
    return [pltpu.with_memory_space_constraint(a, pltpu.HBM) for a in arrays]


def in_vmem(*arrays):
    return [pltpu.with_memory_space_constraint(a, pltpu.VMEM) for a in arrays]


def shift(block, axis, step):
    n = SIZES[axis]
    return lax.ppermute(block, axis, [(i, (i + step) % n) for i in range(n)])


def copies(block, axes):
    n = math.prod(SIZES[a] for a in axes)
    sent = jnp.broadcast_to(block[None], (n,) + block.shape)
    return lax.all_to_all(sent, axes, 0, 0, tiled=True)


def sum_all(tiles):
    parts = lax.all_to_all(tiles, PLANE, 0, 0, tiled=True)
    parts = copies(jnp.sum(parts, 0), ("z",))
    return copies(jnp.sum(parts, 0), PLANE)


def corrected_kernel(
    x_hbm, g_hbm, fb_hbm, basis_hbm, corrected_hbm, tiles_ref,
    x_ref, g_ref, fb_ref, basis_ref, out_ref, x_sem, in_sems, out_sems,
):
    width = g_ref.shape[2]
    fetch_x = pltpu.make_async_copy(x_hbm, x_ref, x_sem)
    fetch_x.start()
    fetches = []
    for q in range(QUARTERS):
        columns = pl.ds(q * width, width)
        pairs = ((g_hbm, g_ref), (fb_hbm, fb_ref), (basis_hbm, basis_ref))
        fetches.append(
            [
                pltpu.make_async_copy(whole.at[:, columns], part.at[q], in_sems.at[q, i])
                for i, (whole, part) in enumerate(pairs)
            ]
        )
        for fetch in fetches[q]:
            fetch.start()
    fetch_x.wait()
    xt = x_ref[...].T

    def factor_part(q):
        return lax.dot_general(
            basis_ref[q].astype(jnp.bfloat16),
            out_ref[q],
            (((1,), (1,)), ((), ())),
            preferred_element_type=jnp.float32,
        )

    parts = []
    stores = []
    for q in range(QUARTERS):
        for fetch in fetches[q]:
            fetch.wait()
        grad = jnp.dot(xt, g_ref[q], preferred_element_type=jnp.float32)
        if q:
            parts.append(factor_part(q - 1))
        grad = grad * (1.0 / math.sqrt(x_ref.shape[0])) + fb_ref[q].astype(jnp.float32)
        out_ref[q] = grad.astype(jnp.bfloat16)
        stores.append(pltpu.make_async_copy(out_ref.at[q], corrected_hbm.at[q], out_sems.at[q]))
        stores[q].start()
    parts.append(factor_part(QUARTERS - 1))
    total = sum(parts[1:], parts[0])
    rows, columns = total.shape
    for i in range(rows // 8):
        for j in range(columns // 128):
            tiles_ref[i * (columns // 128) + j] = total[8 * i : 8 * i + 8, 128 * j : 128 * j + 128]
    for store in stores:
        store.wait()


def corrected_and_factor(layer_input, output_grad, feedback, basis_prev):
    tokens, rows = layer_input.shape
    columns, rank = output_grad.shape[1], basis_prev.shape[0]
    width = columns // QUARTERS
    return pl.pallas_call(
        corrected_kernel,
        in_specs=[pl.BlockSpec(memory_space=pltpu.HBM)] * 4,
        out_specs=[pl.BlockSpec(memory_space=pltpu.HBM), pl.BlockSpec(memory_space=pltpu.VMEM)],
        out_shape=[
            pltpu.HBM((QUARTERS, rows, width), jnp.bfloat16),
            jax.ShapeDtypeStruct((rank * rows // 1024, 8, 128), jnp.float32),
        ],
        scratch_shapes=[
            pltpu.VMEM((tokens, rows), jnp.bfloat16),
            pltpu.VMEM((QUARTERS, tokens, width), jnp.bfloat16),
            pltpu.VMEM((QUARTERS, rows, width), jnp.bfloat16),
            pltpu.VMEM((QUARTERS, rank, width), jnp.float32),
            pltpu.VMEM((QUARTERS, rows, width), jnp.bfloat16),
            pltpu.SemaphoreType.DMA(()),
            pltpu.SemaphoreType.DMA((QUARTERS, 3)),
            pltpu.SemaphoreType.DMA((QUARTERS,)),
        ],
        compiler_params=VMEM,
        name="corrected",
    )(*in_hbm(layer_input, output_grad, feedback, basis_prev))


def eliminate(factor):
    rank, columns = factor.shape
    both = jnp.concatenate([factor, factor], 0)
    gram = lax.dot_general(
        factor,
        both,
        (((1,), (1,)), ((), ())),
        preferred_element_type=jnp.float32,
        precision=lax.Precision.HIGHEST,
    )
    blocks = rank // 8
    lanes = columns // 128
    table = [
        [gram[8 * i : 8 * i + 8]]
        + [factor[8 * i : 8 * i + 8, 128 * j : 128 * j + 128] for j in range(lanes)]
        for i in range(blocks)
    ]
    sublane = lax.broadcasted_iota(jnp.int32, (8, 128), 0)
    spread = lambda row: jnp.broadcast_to(row, (8, 128))
    out = []
    for p in range(blocks):
        below = range(p, blocks)
        col = [
            {i: jnp.broadcast_to(table[i][0][:, 8 * p + j : 8 * p + j + 1], (8, 128)) for i in below}
            for j in range(8)
        ]
        pivots = jnp.ones((8, 128), jnp.float32)
        for j in range(8):
            pivot = spread(col[j][p][j : j + 1])
            pivots = jnp.where(sublane == j, pivot, pivots)
            if p == blocks - 1 and j == 7:
                break
            inverse = 1.0 / pivot
            mult = {i: col[j][i] * inverse for i in below}
            mult[p] = jnp.where(sublane > j, mult[p], 0.0)
            for k in range(j + 1, 8):
                entry = spread(col[j][p][k : k + 1])
                for i in below:
                    col[k][i] = col[k][i] - mult[i] * entry
            for t in range(lanes + 1):
                if t == 0 and p == blocks - 1:
                    continue
                row = spread(table[p][t][j : j + 1])
                for i in below:
                    table[i][t] = table[i][t] - mult[i] * row
        scale = lax.rsqrt(pivots)
        out.append([table[p][t] * scale for t in range(1, lanes + 1)])
    return out


def factor_kernel(me_ref, tiles_ref, corrected_hbm, left_ref, low_ref, *rest):
    term_refs, (corrected_ref, sem) = rest[:QUARTERS], rest[QUARTERS:]
    me = me_ref[0]
    fetch = pltpu.make_async_copy(corrected_hbm, corrected_ref, sem)
    fetch.start()
    rank, columns = left_ref.shape
    lanes = columns // 128
    factor = jnp.concatenate(
        [
            jnp.concatenate([tiles_ref[i * lanes + j] for j in range(lanes)], 1)
            for i in range(rank // 8)
        ],
        0,
    )
    blocks = eliminate(factor)
    for i, block in enumerate(blocks):
        for j, tile in enumerate(block):
            left_ref[8 * i : 8 * i + 8, 128 * j : 128 * j + 128] = tile
    low = left_ref[...].astype(jnp.bfloat16)
    low_ref[...] = low
    fetch.wait()
    for k in range(QUARTERS):
        quarter = lax.rem(me + k, QUARTERS)
        term_refs[k][...] = jnp.dot(low, corrected_ref[quarter], preferred_element_type=jnp.float32)


def factor_and_terms(me, tiles, corrected, rank):
    quarters, rows, width = corrected.shape
    whole = pl.BlockSpec(memory_space=pltpu.VMEM)
    return pl.pallas_call(
        factor_kernel,
        in_specs=[
            pl.BlockSpec(memory_space=pltpu.SMEM),
            whole,
            pl.BlockSpec(memory_space=pltpu.HBM),
        ],
        out_specs=[whole] * (2 + quarters),
        out_shape=[
            jax.ShapeDtypeStruct((rank, rows), jnp.float32),
            jax.ShapeDtypeStruct((rank, rows), jnp.bfloat16),
        ]
        + [jax.ShapeDtypeStruct((rank, width), jnp.float32)] * quarters,
        scratch_shapes=[pltpu.VMEM(corrected.shape, jnp.bfloat16), pltpu.SemaphoreType.DMA(())],
        compiler_params=VMEM,
        name="factor",
    )(me, tiles, *in_hbm(corrected))


def subtract(quarter, total_ref, low_t_ref, corrected_ref, next_hbm, feedback_hbm, next_ref, out_ref, sems):
    rows, width = out_ref.shape
    height = rows // STRIPS
    columns = pl.ds(pl.multiple_of(quarter * width, 128), width)
    basis_next = total_ref[...] * (1.0 / REPLICAS)
    next_ref[...] = basis_next
    stores = [pltpu.make_async_copy(next_ref, next_hbm.at[:, columns], sems.at[STRIPS])]
    stores[0].start()
    basis_round = basis_next.astype(jnp.bfloat16)
    for i in range(STRIPS):
        strip = pl.ds(i * height, height)
        approx = jnp.dot(low_t_ref[strip], basis_round, preferred_element_type=jnp.float32)
        out_ref[strip] = (corrected_ref[strip].astype(jnp.float32) - approx).astype(jnp.bfloat16)
        stores.append(
            pltpu.make_async_copy(out_ref.at[strip], feedback_hbm.at[strip, columns], sems.at[i])
        )
        stores[-1].start()
    return stores


def own_quarter_kernel(
    me_ref, total_ref, low_t_ref, corrected_hbm, next_hbm, feedback_hbm, *rest
):
    other_refs, (next_ref, out_ref, own_ref, sems, fetch_sems) = rest[: QUARTERS - 1], rest[QUARTERS - 1 :]
    me = me_ref[0]
    places = [own_ref] + list(other_refs)
    fetches = [
        pltpu.make_async_copy(
            corrected_hbm.at[lax.rem(me + (QUARTERS - k), QUARTERS)], places[k], fetch_sems.at[k]
        )
        for k in range(QUARTERS)
    ]
    for k in ARRIVING:
        fetches[k].start()
    fetches[0].wait()
    stores = subtract(me, total_ref, low_t_ref, own_ref, next_hbm, feedback_hbm, next_ref, out_ref, sems)
    for k in ARRIVING[1:]:
        fetches[k].wait()
    for store in stores:
        store.wait()


def other_quarter_kernel(
    me_ref, total_ref, low_t_ref, corrected_ref, next_in, feedback_in, next_hbm, feedback_hbm, next_ref, out_ref, sems, *, k
):
    quarter = lax.rem(me_ref[0] + (QUARTERS - k), QUARTERS)
    for store in subtract(
        quarter, total_ref, low_t_ref, corrected_ref, next_hbm, feedback_hbm, next_ref, out_ref, sems
    ):
        store.wait()


def finish(me, totals, low_t, corrected):
    quarters, rows, width = corrected.shape
    rank = low_t.shape[1]
    hbm = pl.BlockSpec(memory_space=pltpu.HBM)
    whole = pl.BlockSpec(memory_space=pltpu.VMEM)
    scalar = pl.BlockSpec(memory_space=pltpu.SMEM)
    outputs = [
        pltpu.HBM((rank, width * quarters), jnp.float32),
        pltpu.HBM((rows, width * quarters), jnp.bfloat16),
    ]
    scratch = [
        pltpu.VMEM((rank, width), jnp.float32),
        pltpu.VMEM((rows, width), jnp.bfloat16),
    ]
    *results, first, second, third = pl.pallas_call(
        own_quarter_kernel,
        in_specs=[scalar, whole, whole, hbm],
        out_specs=[hbm, hbm] + [whole] * (quarters - 1),
        out_shape=outputs + [pltpu.VMEM((rows, width), jnp.bfloat16)] * (quarters - 1),
        scratch_shapes=scratch
        + [
            pltpu.VMEM((rows, width), jnp.bfloat16),
            pltpu.SemaphoreType.DMA((STRIPS + 1,)),
            pltpu.SemaphoreType.DMA((quarters,)),
        ],
        compiler_params=VMEM,
        name="own_quarter",
    )(me, totals[0], low_t, *in_hbm(corrected))
    blocks = [None, first, second, third]
    for k in ARRIVING[1:]:
        results = pl.pallas_call(
            functools.partial(other_quarter_kernel, k=k),
            in_specs=[scalar, whole, whole, whole, hbm, hbm],
            out_specs=[hbm, hbm],
            out_shape=outputs,
            scratch_shapes=scratch + [pltpu.SemaphoreType.DMA((STRIPS + 1,))],
            input_output_aliases={4: 0, 5: 1},
            compiler_params=VMEM,
            name="quarter",
        )(me, totals[k], low_t, *in_vmem(blocks[k]), *in_hbm(*results))
    return results


def local(layer_input, output_grad, feedback, basis_prev):
    me = lax.axis_index("x").reshape(1)
    corrected, tiles = corrected_and_factor(layer_input, output_grad, feedback, basis_prev)
    tiles, me = lax.optimization_barrier((tiles, me))
    tiles = sum_all(tiles)
    factor_left, factor_low, *terms = factor_and_terms(me, tiles, corrected, basis_prev.shape[0])
    factor_low_t = factor_low.T

    arrived = [shift(terms[k], "x", k) for k in range(1, QUARTERS)]
    quarter = terms[0] + sum(arrived)
    piece = lax.all_to_all(quarter.reshape(SIZES["z"], 8, -1), "z", 0, 0, tiled=True)
    piece = jnp.sum(piece, 0)
    quarter = copies(piece, ("z",)).reshape(quarter.shape)
    totals = [quarter] + [shift(quarter, "x", k) for k in range(1, QUARTERS)]
    results = finish(me, totals, factor_low_t, corrected)
    return (factor_left,) + tuple(results)


def solution(mesh):
    fine = Mesh(mesh.devices.reshape(8, 4, 4, 2), ("z", "x", "y", "c"))
    dp, tensor = ("z", "x"), ("y", "c")
    in_specs = (P(dp, None), P(dp, tensor), P(dp, tensor), P(None, tensor))
    out_specs = (P(), P(None, tensor), P(dp, tensor))
    return jax.shard_map(local, mesh=fine, in_specs=in_specs, out_specs=out_specs, check_vma=False)
```

time: 117 us -> 110 us (0.940)
  the two profiles are of different devices: /device:TPU:8 before, /device:TPU:6 now
where the time goes in v3:
time: 110 us; the launch traced here: 109 us
  blocking collectives  68.4 us (62%)
  waiting for transfers between devices  17.3 us (16%)
  Pallas kernels  16.4 us (15%)
  starting transfers between devices  6.32 us (6%)
    all_to_all x3, blocking collectives, copies(): return lax.all_to_all(sent, axes, 0, 0, tiled=True)  41 us
    ppermute x6, waiting for transfers between devices, shift(): return lax.ppermute(block, axis, [(i, (i + step) % n) for i in range(n)])  17.3 us
    all_to_all x1, blocking collectives, local(): lax.all_to_all(quarter.reshape(SIZES['z'], 8, -1), 'z', 0, 0, tiled=True)  14 us
    all_to_all x1, blocking collectives, sum_all(): parts = lax.all_to_all(tiles, PLANE, 0, 0, tiled=True)  13.3 us
    ppermute x6, starting transfers between devices, shift(): return lax.ppermute(block, axis, [(i, (i + step) % n) for i in range(n)])  6.32 us
    pallas_call x1, Pallas kernels, corrected_and_factor(): pl.pallas_call(corrected_kernel, in_specs=[pl.BlockSpec(memory_space=pltp...  6.02 us
    pallas_call x1, Pallas kernels, factor_and_terms(): pl.pallas_call(factor_kernel, in_specs=[pl.BlockSpec(memory_space=pltpu.S...  4.44 us
    pallas_call x3, Pallas kernels, finish(): pl.pallas_call(functools.partial(other_quarter_kernel, k=k), in_specs=[sc...  3.51 us
  transfers between devices with their start and end apart: 6, of which 4 were waited for; matrix products, arithmetic and copies ran while one was open for 0% of the time, Pallas kernels for 4%

profile of v3, /device:TPU:6, one launch (start us, length us, event | category | flops | bytes accessed | tf_op | source)
XLA Modules:
  0.0 109.4 jit_solution(523601551789744096)
XLA Ops:
  0.6 6.0 %corrected.1 = (bf16[4,512,896]{2,1,0:T(8,128)(2,1)}, f32[32,8,128]{2,1,0:T(8,128)S(1)}) custom-call(bf16[256,512]{1,0:T(8,128)(2,1)} %x_hbm.1, bf16[256,3584]{1,0:T(8,128)(2,1)} %g_hbm.1, bf16[512,3584]{1,0:T(8,128)(2,1)} %fb_hbm.1, f32[64,3584]{1,0:T(8,128)} %basis_hbm.1), custom_call_target="tpu_custom_call" | custom-call | tf_op jit(solution)/shard_map/corrected/pallas_call | solution.py:102
  6.7 13.3 %all_to_all.25 = f32[32,8,128]{2,1,0:T(8,128)S(1)} all-to-all(f32[32,8,128]{2,1,0:T(8,128)S(1)} %get-tuple-element.26), channel_id=1, replica_groups=mesh['z'=8,'x'=4,'y'=4,'c'=2] {'x','y','c'}, dimensions={0} | all-to-all | bytes 262144 | tf_op jit(solution)/shard_map/all_to_all | solution.py:41
  20.0 16.3 %all_to_all.26 = f32[8,8,128]{2,1,0:T(8,128)S(1)} all-to-all(f32[8,8,128]{2,1,0:T(8,128)S(1)} %broadcast_in_dim.6), channel_id=1, replica_groups=mesh['z'=8,'x'=4,'y'=4,'c'=2] {'z'}, dimensions={0} | all-to-all | bytes 65536 | tf_op jit(solution)/shard_map/all_to_all | solution.py:37
  36.3 11.3 %all_to_all.27.tiles_ref = f32[32,8,128]{2,1,0:T(8,128)S(1)} all-to-all(f32[32,8,128]{2,1,0:T(8,128)S(1)} %broadcast_in_dim.7), channel_id=1, replica_groups=mesh['z'=8,'x'=4,'y'=4,'c'=2] {'x','y','c'}, dimensions={0} | all-to-all | bytes 262144 | tf_op jit(solution)/shard_map/all_to_all | solution.py:37
  47.6 4.4 %factor.1 = (f32[64,512]{1,0:T(8,128)}, bf16[64,512]{1,0:T(8,128)(2,1)S(1)}, f32[64,896]{1,0:T(8,128)S(1)}, f32[64,896]{1,0:T(8,128)S(1)}, f32[64,896]{1,0:T(8,128)S(1)}, /*index=5*/f32[64,896]{1,0:T(8,128)S(1)}) custom-call(s32[1]{0:T(128)} %bitcast.me_ref, f32[32,8,128]{2,1,0:T(8,128)S(1)} %all_to_all.27.tiles_ref, ...), custom_call_target="tpu_custom_call" | custom-call | tf_op jit(solution)/shard_map/factor/pallas_call | solution.py:204
  52.1 2.2 %collective-permute-start = (f32[64,896]{1,0:T(8,128)S(1)}, f32[64,896]{1,0:T(8,128)S(1)}, u32[]{:S(2)}, u32[]{:S(2)}) collective-permute-start(f32[64,896]{1,0:T(8,128)S(1)} %get-tuple-element.30), channel_id=1, source_target_pairs={{0,8},{8,16},{16,24},{24,0},{1,9},{9,17},{17,25},{25,1},{2,10},{10... | collective-permute-start | bytes 688136 | tf_op jit(solution)/shard_map/ppermute | solution.py:31
  54.3 0.7 collective-permute-start.1
  54.9 0.8 collective-permute-start.2
  55.7 8.7 %collective-permute-done = f32[64,896]{1,0:T(8,128)S(1)} collective-permute-done((f32[64,896]{1,0:T(8,128)S(1)}, f32[64,896]{1,0:T(8,128)S(1)}, u32[]{:S(2)}, u32[]{:S(2)}) %collective-permute-start) | collective-permute-done | bytes 229408 | tf_op jit(solution)/shard_map/ppermute | solution.py:31
  64.4 0.0 collective-permute-done.1
  64.4 3.7 %collective-permute-done.2 = f32[64,896]{1,0:T(8,128)S(1)} collective-permute-done((f32[64,896]{1,0:T(8,128)S(1)}, f32[64,896]{1,0:T(8,128)S(1)}, u32[]{:S(2)}, u32[]{:S(2)}) %collective-permute-start.2) | collective-permute-done | bytes 229408 | tf_op jit(solution)/shard_map/ppermute | solution.py:31
  68.0 0.1 add_bitcast_fusion
  68.1 14.0 %all_to_all.28 = f32[8,8,896]{2,1,0:T(8,128)S(1)} all-to-all(f32[8,8,896]{2,1,0:T(8,128)S(1)} %add_bitcast_fusion), channel_id=1, replica_groups=mesh['z'=8,'x'=4,'y'=4,'c'=2] {'z'}, dimensions={0} | all-to-all | bytes 458752 | tf_op jit(solution)/shard_map/all_to_all | solution.py:328
  82.2 13.5 %all_to_all.29 = f32[8,8,896]{2,1,0:T(8,128)S(1)} all-to-all(f32[8,8,896]{2,1,0:T(8,128)S(1)} %broadcast_in_dim.8), channel_id=1, replica_groups=mesh['z'=8,'x'=4,'y'=4,'c'=2] {'z'}, dimensions={0} | all-to-all | bytes 458752 | tf_op jit(solution)/shard_map/all_to_all | solution.py:37
  95.7 2.0 %collective-permute-start.4 = (f32[64,896]{1,0:T(8,128)S(1)}, f32[64,896]{1,0:T(8,128)S(1)}, u32[]{:S(2)}, u32[]{:S(2)}) collective-permute-start(f32[64,896]{1,0:T(8,128)S(1)} %bitcast.10), channel_id=1, source_target_pairs={{0,24},{8,0},{16,8},{24,16},{1,25},{9,1},{17,9},{25,17},{2,26},{10... | collective-permute-start | bytes 688136 | tf_op jit(solution)/shard_map/ppermute | solution.py:31
  97.7 0.7 collective-permute-start.3
  98.3 0.1 copy.14
  98.5 2.4 %own_quarter.1 = (f32[64,3584]{1,0:T(8,128)}, bf16[512,3584]{1,0:T(8,128)(2,1)}, bf16[512,896]{1,0:T(8,128)(2,1)S(1)}, bf16[512,896]{1,0:T(8,128)(2,1)S(1)}, bf16[512,896]{1,0:T(8,128)(2,1)S(1)}) custom-call(s32[1]{0:T(128)} %bitcast.me_ref, f32[64,896]{1,0:T(8,128)S(1)} %bitcast.12, bf16[512,64]{1,0:T(8,128)(2,1)S(1)} %bitcast.5, ...), custom_call_target="tpu_custom_call" | custom-call | tf_op jit(solution)/shard_map/own_quarter/pallas_call | solution.py:289
  100.9 2.5 %collective-permute-done.5.total_ref = f32[64,896]{1,0:T(8,128)S(1)} collective-permute-done((f32[64,896]{1,0:T(8,128)S(1)}, f32[64,896]{1,0:T(8,128)S(1)}, u32[]{:S(2)}, u32[]{:S(2)}) %collective-permute-start.5) | collective-permute-done | bytes 229408 | tf_op jit(solution)/shard_map/ppermute | solution.py:31
  103.4 1.2 %quarter.3 = (f32[64,3584]{1,0:T(8,128)}, bf16[512,3584]{1,0:T(8,128)(2,1)}) custom-call(s32[1]{0:T(128)} %bitcast.me_ref, f32[64,896]{1,0:T(8,128)S(1)} %collective-permute-done.5.total_ref, bf16[512,64]{1,0:T(8,128)(2,1)S(1)} %bitcast.6, bf16[512,896]{1,0:T(8,128)(2,1)S(1)} %get-tuple-element.36.corrected_ref, ...), custom_call_target="tpu_custom_call", output_to_operand_aliasing={{0}: (4, {}), {1}: (5, {})} | custom-call | tf_op jit(solution)/shard_map/quarter/pallas_call | solution.py:305
  104.5 2.5 %collective-permute-done.4.total_ref = f32[64,896]{1,0:T(8,128)S(1)} collective-permute-done((f32[64,896]{1,0:T(8,128)S(1)}, f32[64,896]{1,0:T(8,128)S(1)}, u32[]{:S(2)}, u32[]{:S(2)}) %collective-permute-start.4) | collective-permute-done | bytes 229408 | tf_op jit(solution)/shard_map/ppermute | solution.py:31
  107.0 1.2 %quarter.4 = (f32[64,3584]{1,0:T(8,128)}, bf16[512,3584]{1,0:T(8,128)(2,1)}) custom-call(s32[1]{0:T(128)} %bitcast.me_ref, f32[64,896]{1,0:T(8,128)S(1)} %collective-permute-done.4.total_ref, bf16[512,64]{1,0:T(8,128)(2,1)S(1)} %bitcast.7, bf16[512,896]{1,0:T(8,128)(2,1)S(1)} %get-tuple-element.35.corrected_ref, ...), custom_call_target="tpu_custom_call", output_to_operand_aliasing={{0}: (4, {}), {1}: (5, {})} | custom-call | tf_op jit(solution)/shard_map/quarter/pallas_call | solution.py:305
  108.2 0.0 collective-permute-done.3.total_ref
  108.2 1.2 %quarter.5 = (f32[64,3584]{1,0:T(8,128)}, bf16[512,3584]{1,0:T(8,128)(2,1)}) custom-call(s32[1]{0:T(128)} %bitcast.me_ref, f32[64,896]{1,0:T(8,128)S(1)} %collective-permute-done.3.total_ref, bf16[512,64]{1,0:T(8,128)(2,1)S(1)} %bitcast.8, bf16[512,896]{1,0:T(8,128)(2,1)S(1)} %get-tuple-element.34.corrected_ref, ...), custom_call_target="tpu_custom_call", output_to_operand_aliasing={{0}: (4, {}), {1}: (5, {})} | custom-call | tf_op jit(solution)/shard_map/quarter/pallas_call | solution.py:305
  (7 shorter events, 0.1 us)
Async XLA Ops:
  52.1 12.3 %collective-permute-start = (f32[64,896]{1,0:T(8,128)S(1)}, f32[64,896]{1,0:T(8,128)S(1)}, u32[]{:S(2)}, u32[]{:S(2)}) collective-permute-start(f32[64,896]{1,0:T(8,128)S(1)} %get-tuple-element.30), channel_id=1, source_target_pairs={{0,8},{8,16},{16,24},{24,0},{1,9},{9,17},{17,25},{25,1},{2,10},{10... | collective-permute-start | bytes 688136 | tf_op jit(solution)/shard_map/ppermute | solution.py:31
  54.3 10.1 %collective-permute-start.1 = (f32[64,896]{1,0:T(8,128)S(1)}, f32[64,896]{1,0:T(8,128)S(1)}, u32[]{:S(2)}, u32[]{:S(2)}) collective-permute-start(f32[64,896]{1,0:T(8,128)S(1)} %get-tuple-element.31), channel_id=1, source_target_pairs={{0,16},{8,24},{16,0},{24,8},{1,17},{9,25},{17,1},{25,9},{2,18},{10... | collective-permute-start | bytes 688136 | tf_op jit(solution)/shard_map/ppermute | solution.py:31
  54.9 13.1 %collective-permute-start.2 = (f32[64,896]{1,0:T(8,128)S(1)}, f32[64,896]{1,0:T(8,128)S(1)}, u32[]{:S(2)}, u32[]{:S(2)}) collective-permute-start(f32[64,896]{1,0:T(8,128)S(1)} %get-tuple-element.32), channel_id=1, source_target_pairs={{0,24},{8,0},{16,8},{24,16},{1,25},{9,1},{17,9},{25,17},{2,26},{10... | collective-permute-start | bytes 688136 | tf_op jit(solution)/shard_map/ppermute | solution.py:31
  95.7 7.7 %collective-permute-start.5 = (f32[64,896]{1,0:T(8,128)S(1)}, f32[64,896]{1,0:T(8,128)S(1)}, u32[]{:S(2)}, u32[]{:S(2)}) collective-permute-start(f32[64,896]{1,0:T(8,128)S(1)} %bitcast.9), channel_id=1, source_target_pairs={{0,8},{8,16},{16,24},{24,0},{1,9},{9,17},{17,25},{25,1},{2,10},{10... | collective-permute-start | bytes 688136 | tf_op jit(solution)/shard_map/ppermute | solution.py:31
  95.7 11.4 %collective-permute-start.4 = (f32[64,896]{1,0:T(8,128)S(1)}, f32[64,896]{1,0:T(8,128)S(1)}, u32[]{:S(2)}, u32[]{:S(2)}) collective-permute-start(f32[64,896]{1,0:T(8,128)S(1)} %bitcast.10), channel_id=1, source_target_pairs={{0,24},{8,0},{16,8},{24,16},{1,25},{9,1},{17,9},{25,17},{2,26},{10... | collective-permute-start | bytes 688136 | tf_op jit(solution)/shard_map/ppermute | solution.py:31
  97.7 10.5 %collective-permute-start.3 = (f32[64,896]{1,0:T(8,128)S(1)}, f32[64,896]{1,0:T(8,128)S(1)}, u32[]{:S(2)}, u32[]{:S(2)}) collective-permute-start(f32[64,896]{1,0:T(8,128)S(1)} %bitcast.11), channel_id=1, source_target_pairs={{0,16},{8,24},{16,0},{24,8},{1,17},{9,25},{17,1},{25,9},{2,18},{10... | collective-permute-start | bytes 688136 | tf_op jit(solution)/shard_map/ppermute | solution.py:31

commit v4 on v3

--- a/solution.py
+++ b/solution.py
@@ -1,4 +1,3 @@
-import functools
 import math
 
 import jax
@@ -9,13 +8,15 @@
 from jax.sharding import Mesh
 from jax.sharding import PartitionSpec as P
 
-SIZES = dict(z=8, x=4, y=4, c=2)
+SIZES = dict(zh=4, zl=2, x=4, y=4, c=2)
 PLANE = ("x", "y", "c")
-REPLICAS = SIZES["z"] * SIZES["x"]
+LINE = ("zh", "zl")
+NEAR = ("zl", "x")
+REPLICAS = SIZES["zh"] * SIZES["zl"] * SIZES["x"]
 QUARTERS = SIZES["x"]
-STRIPS = 4
-ARRIVING = (0, 1, 3, 2)
-VMEM = pltpu.CompilerParams(vmem_limit_bytes=24 << 20)
+HALVES = SIZES["zl"]
+EARLY = 2
+VMEM = pltpu.CompilerParams(vmem_limit_bytes=20 << 20)
 
 
 def in_hbm(*arrays):
@@ -39,7 +40,7 @@
 
 def sum_all(tiles):
     parts = lax.all_to_all(tiles, PLANE, 0, 0, tiled=True)
-    parts = copies(jnp.sum(parts, 0), ("z",))
+    parts = copies(jnp.sum(parts, 0), LINE)
     return copies(jnp.sum(parts, 0), PLANE)
 
 
@@ -172,9 +173,7 @@
     return out
 
 
-def factor_kernel(me_ref, tiles_ref, corrected_hbm, left_ref, low_ref, *rest):
-    term_refs, (corrected_ref, sem) = rest[:QUARTERS], rest[QUARTERS:]
-    me = me_ref[0]
+def factor_kernel(tiles_ref, corrected_hbm, left_ref, low_ref, terms_ref, corrected_ref, sem):
     fetch = pltpu.make_async_copy(corrected_hbm, corrected_ref, sem)
     fetch.start()
     rank, columns = left_ref.shape
@@ -193,149 +192,126 @@
     low = left_ref[...].astype(jnp.bfloat16)
     low_ref[...] = low
     fetch.wait()
-    for k in range(QUARTERS):
-        quarter = lax.rem(me + k, QUARTERS)
-        term_refs[k][...] = jnp.dot(low, corrected_ref[quarter], preferred_element_type=jnp.float32)
-
-
-def factor_and_terms(me, tiles, corrected, rank):
+    for q in range(QUARTERS):
+        term = jnp.dot(low, corrected_ref[q], preferred_element_type=jnp.float32)
+        for h in range(HALVES):
+            terms_ref[h * QUARTERS + q] = term[h * (rank // HALVES) : (h + 1) * (rank // HALVES)]
+
+
+def factor_and_terms(tiles, corrected, rank):
     quarters, rows, width = corrected.shape
     whole = pl.BlockSpec(memory_space=pltpu.VMEM)
     return pl.pallas_call(
         factor_kernel,
-        in_specs=[
-            pl.BlockSpec(memory_space=pltpu.SMEM),
-            whole,
-            pl.BlockSpec(memory_space=pltpu.HBM),
-        ],
-        out_specs=[whole] * (2 + quarters),
+        in_specs=[whole, pl.BlockSpec(memory_space=pltpu.HBM)],
+        out_specs=[whole] * 3,
         out_shape=[
             jax.ShapeDtypeStruct((rank, rows), jnp.float32),
             jax.ShapeDtypeStruct((rank, rows), jnp.bfloat16),
-        ]
-        + [jax.ShapeDtypeStruct((rank, width), jnp.float32)] * quarters,
+            jax.ShapeDtypeStruct((HALVES * quarters, rank // HALVES, width), jnp.float32),
+        ],
         scratch_shapes=[pltpu.VMEM(corrected.shape, jnp.bfloat16), pltpu.SemaphoreType.DMA(())],
         compiler_params=VMEM,
         name="factor",
-    )(me, tiles, *in_hbm(corrected))
-
-
-def subtract(quarter, total_ref, low_t_ref, corrected_ref, next_hbm, feedback_hbm, next_ref, out_ref, sems):
-    rows, width = out_ref.shape
-    height = rows // STRIPS
-    columns = pl.ds(pl.multiple_of(quarter * width, 128), width)
-    basis_next = total_ref[...] * (1.0 / REPLICAS)
-    next_ref[...] = basis_next
-    stores = [pltpu.make_async_copy(next_ref, next_hbm.at[:, columns], sems.at[STRIPS])]
-    stores[0].start()
-    basis_round = basis_next.astype(jnp.bfloat16)
-    for i in range(STRIPS):
-        strip = pl.ds(i * height, height)
-        approx = jnp.dot(low_t_ref[strip], basis_round, preferred_element_type=jnp.float32)
-        out_ref[strip] = (corrected_ref[strip].astype(jnp.float32) - approx).astype(jnp.bfloat16)
-        stores.append(
-            pltpu.make_async_copy(out_ref.at[strip], feedback_hbm.at[strip, columns], sems.at[i])
+    )(tiles, *in_hbm(corrected))
+
+
+def fetch_kernel(after_ref, low_ref, corrected_hbm, low_t_ref, fetched_ref, sem):
+    fetch = pltpu.make_async_copy(corrected_hbm.at[pl.ds(0, EARLY)], fetched_ref, sem)
+    fetch.start()
+    low_t_ref[...] = low_ref[...].astype(jnp.float32).T.astype(jnp.bfloat16)
+    fetch.wait()
+
+
+def fetch_after(before, low, corrected):
+    rank, rows = low.shape
+    whole = pl.BlockSpec(memory_space=pltpu.VMEM)
+    return pl.pallas_call(
+        fetch_kernel,
+        in_specs=[pl.BlockSpec(memory_space=pl.ANY), whole, pl.BlockSpec(memory_space=pltpu.HBM)],
+        out_specs=[whole, whole],
+        out_shape=[
+            pltpu.VMEM((rows, rank), low.dtype),
+            pltpu.VMEM((EARLY,) + corrected.shape[1:], corrected.dtype),
+        ],
+        scratch_shapes=[pltpu.SemaphoreType.DMA(())],
+        compiler_params=VMEM,
+        name="fetch",
+    )(before, low, *in_hbm(corrected))
+
+
+def feedback_kernel(
+    total_ref, low_t_ref, early_ref, corrected_hbm, next_hbm, feedback_hbm, next_ref, out_ref, late_ref, sems, late_sems
+):
+    quarters, rows, width = out_ref.shape
+    fetches = [
+        pltpu.make_async_copy(corrected_hbm.at[q], late_ref.at[q - EARLY], late_sems.at[q - EARLY])
+        for q in range(EARLY, quarters)
+    ]
+    for fetch in fetches:
+        fetch.start()
+    stores = []
+    for q in range(quarters):
+        columns = pl.ds(q * width, width)
+        basis_next = jnp.concatenate([total_ref[h * quarters + q] for h in range(HALVES)], 0) * (1.0 / REPLICAS)
+        next_ref[q] = basis_next
+        stores.append(pltpu.make_async_copy(next_ref.at[q], next_hbm.at[:, columns], sems.at[0, q]))
+        stores[-1].start()
+        approx = jnp.dot(
+            low_t_ref[...], basis_next.astype(jnp.bfloat16), preferred_element_type=jnp.float32
         )
+        if q >= EARLY:
+            fetches[q - EARLY].wait()
+        corrected = early_ref[q] if q < EARLY else late_ref[q - EARLY]
+        out_ref[q] = (corrected.astype(jnp.float32) - approx).astype(jnp.bfloat16)
+        stores.append(pltpu.make_async_copy(out_ref.at[q], feedback_hbm.at[:, columns], sems.at[1, q]))
         stores[-1].start()
-    return stores
-
-
-def own_quarter_kernel(
-    me_ref, total_ref, low_t_ref, corrected_hbm, next_hbm, feedback_hbm, *rest
-):
-    other_refs, (next_ref, out_ref, own_ref, sems, fetch_sems) = rest[: QUARTERS - 1], rest[QUARTERS - 1 :]
-    me = me_ref[0]
-    places = [own_ref] + list(other_refs)
-    fetches = [
-        pltpu.make_async_copy(
-            corrected_hbm.at[lax.rem(me + (QUARTERS - k), QUARTERS)], places[k], fetch_sems.at[k]
-        )
-        for k in range(QUARTERS)
-    ]
-    for k in ARRIVING:
-        fetches[k].start()
-    fetches[0].wait()
-    stores = subtract(me, total_ref, low_t_ref, own_ref, next_hbm, feedback_hbm, next_ref, out_ref, sems)
-    for k in ARRIVING[1:]:
-        fetches[k].wait()
     for store in stores:
         store.wait()
 
 
-def other_quarter_kernel(
-    me_ref, total_ref, low_t_ref, corrected_ref, next_in, feedback_in, next_hbm, feedback_hbm, next_ref, out_ref, sems, *, k
-):
-    quarter = lax.rem(me_ref[0] + (QUARTERS - k), QUARTERS)
-    for store in subtract(
-        quarter, total_ref, low_t_ref, corrected_ref, next_hbm, feedback_hbm, next_ref, out_ref, sems
-    ):
-        store.wait()
-
-
-def finish(me, totals, low_t, corrected):
+def finish(total, low_t, early, corrected):
     quarters, rows, width = corrected.shape
     rank = low_t.shape[1]
     hbm = pl.BlockSpec(memory_space=pltpu.HBM)
     whole = pl.BlockSpec(memory_space=pltpu.VMEM)
-    scalar = pl.BlockSpec(memory_space=pltpu.SMEM)
-    outputs = [
-        pltpu.HBM((rank, width * quarters), jnp.float32),
-        pltpu.HBM((rows, width * quarters), jnp.bfloat16),
-    ]
-    scratch = [
-        pltpu.VMEM((rank, width), jnp.float32),
-        pltpu.VMEM((rows, width), jnp.bfloat16),
-    ]
-    *results, first, second, third = pl.pallas_call(
-        own_quarter_kernel,
-        in_specs=[scalar, whole, whole, hbm],
-        out_specs=[hbm, hbm] + [whole] * (quarters - 1),
-        out_shape=outputs + [pltpu.VMEM((rows, width), jnp.bfloat16)] * (quarters - 1),
-        scratch_shapes=scratch
-        + [
-            pltpu.VMEM((rows, width), jnp.bfloat16),
-            pltpu.SemaphoreType.DMA((STRIPS + 1,)),
-            pltpu.SemaphoreType.DMA((quarters,)),
+    return pl.pallas_call(
+        feedback_kernel,
+        in_specs=[whole, whole, whole, hbm],
+        out_specs=[hbm, hbm],
+        out_shape=[
+            pltpu.HBM((rank, width * quarters), jnp.float32),
+            pltpu.HBM((rows, width * quarters), jnp.bfloat16),
+        ],
+        scratch_shapes=[
+            pltpu.VMEM((quarters, rank, width), jnp.float32),
+            pltpu.VMEM((quarters, rows, width), jnp.bfloat16),
+            pltpu.VMEM((quarters - EARLY, rows, width), jnp.bfloat16),
+            pltpu.SemaphoreType.DMA((2, quarters)),
+            pltpu.SemaphoreType.DMA((quarters - EARLY,)),
         ],
         compiler_params=VMEM,
-        name="own_quarter",
-    )(me, totals[0], low_t, *in_hbm(corrected))
-    blocks = [None, first, second, third]
-    for k in ARRIVING[1:]:
-        results = pl.pallas_call(
-            functools.partial(other_quarter_kernel, k=k),
-            in_specs=[scalar, whole, whole, whole, hbm, hbm],
-            out_specs=[hbm, hbm],
-            out_shape=outputs,
-            scratch_shapes=scratch + [pltpu.SemaphoreType.DMA((STRIPS + 1,))],
-            input_output_aliases={4: 0, 5: 1},
-            compiler_params=VMEM,
-            name="quarter",
-        )(me, totals[k], low_t, *in_vmem(blocks[k]), *in_hbm(*results))
-    return results
+        name="feedback",
+    )(total, *in_vmem(low_t, early), *in_hbm(corrected))
 
 
 def local(layer_input, output_grad, feedback, basis_prev):
-    me = lax.axis_index("x").reshape(1)
     corrected, tiles = corrected_and_factor(layer_input, output_grad, feedback, basis_prev)
-    tiles, me = lax.optimization_barrier((tiles, me))
     tiles = sum_all(tiles)
-    factor_left, factor_low, *terms = factor_and_terms(me, tiles, corrected, basis_prev.shape[0])
-    factor_low_t = factor_low.T
-
-    arrived = [shift(terms[k], "x", k) for k in range(1, QUARTERS)]
-    quarter = terms[0] + sum(arrived)
-    piece = lax.all_to_all(quarter.reshape(SIZES["z"], 8, -1), "z", 0, 0, tiled=True)
-    piece = jnp.sum(piece, 0)
-    quarter = copies(piece, ("z",)).reshape(quarter.shape)
-    totals = [quarter] + [shift(quarter, "x", k) for k in range(1, QUARTERS)]
-    results = finish(me, totals, factor_low_t, corrected)
-    return (factor_left,) + tuple(results)
+    factor_left, factor_low, terms = factor_and_terms(tiles, corrected, basis_prev.shape[0])
+
+    block = jnp.sum(lax.all_to_all(terms, NEAR, 0, 0, tiled=True), 0)
+    one, two, three = (shift(block, "zh", k) for k in (1, 2, 3))
+    low_t, early = fetch_after(block, factor_low, corrected)
+    block = (block + two) + (one + three)
+    block, low_t, early = lax.optimization_barrier((block, low_t, early))
+    basis_next, feedback_next = finish(copies(block, NEAR), low_t, early, corrected)
+    return factor_left, basis_next, feedback_next
 
 
 def solution(mesh):
-    fine = Mesh(mesh.devices.reshape(8, 4, 4, 2), ("z", "x", "y", "c"))
-    dp, tensor = ("z", "x"), ("y", "c")
+    fine = Mesh(mesh.devices.reshape(4, 2, 4, 4, 2), ("zh", "zl", "x", "y", "c"))
+    dp, tensor = ("zh", "zl", "x"), ("y", "c")
     in_specs = (P(dp, None), P(dp, tensor), P(dp, tensor), P(None, tensor))
     out_specs = (P(), P(None, tensor), P(dp, tensor))
     return jax.shard_map(local, mesh=fine, in_specs=in_specs, out_specs=out_specs, check_vma=False)

time: 110 us -> 105 us (0.955)
  the two profiles are of different devices: /device:TPU:6 before, /device:TPU:64 now
where the time goes in v4:
time: 105 us; the launch traced here: 104 us
  blocking collectives  73.5 us (70%)
  Pallas kernels  15.9 us (15%)
  starting transfers between devices  7.08 us (7%)
  waiting for transfers between devices  6.76 us (6%)
    all_to_all x3, blocking collectives, copies(): return lax.all_to_all(sent, axes, 0, 0, tiled=True)  41.2 us
    all_to_all x1, blocking collectives, local(): block = jnp.sum(lax.all_to_all(terms, NEAR, 0, 0, tiled=True), 0)  17.3 us
    all_to_all x1, blocking collectives, sum_all(): parts = lax.all_to_all(tiles, PLANE, 0, 0, tiled=True)  15 us
    ppermute x3, starting transfers between devices, shift(): return lax.ppermute(block, axis, [(i, (i + step) % n) for i in range(n)])  7.08 us
    ppermute x3, waiting for transfers between devices, shift(): return lax.ppermute(block, axis, [(i, (i + step) % n) for i in range(n)])  6.76 us
    pallas_call x1, Pallas kernels, corrected_and_factor(): pl.pallas_call(corrected_kernel, in_specs=[pl.BlockSpec(memory_space=pltp...  6.02 us
    pallas_call x1, Pallas kernels, factor_and_terms(): pl.pallas_call(factor_kernel, in_specs=[whole, pl.BlockSpec(memory_space=...  4.9 us
    pallas_call x1, Pallas kernels, finish(): pl.pallas_call(feedback_kernel, in_specs=[whole, whole, whole, hbm], out_...  3.49 us
  transfers between devices with their start and end apart: 3, of which 3 were waited for; matrix products, arithmetic and copies ran while one was open for 0% of the time, Pallas kernels for 1%

profile of v4, /device:TPU:64, one launch (start us, length us, event | category | flops | bytes accessed | tf_op | source)
XLA Modules:
  0.0 104.1 jit_solution(6966639630135402940)
XLA Ops:
  0.6 6.0 %corrected.1 = (bf16[4,512,896]{2,1,0:T(8,128)(2,1)}, f32[32,8,128]{2,1,0:T(8,128)S(1)}) custom-call(bf16[256,512]{1,0:T(8,128)(2,1)} %x_hbm.1, bf16[256,3584]{1,0:T(8,128)(2,1)} %g_hbm.1, bf16[512,3584]{1,0:T(8,128)(2,1)} %fb_hbm.1, f32[64,3584]{1,0:T(8,128)} %basis_hbm.1), custom_call_target="tpu_custom_call" | custom-call | tf_op jit(solution)/shard_map/corrected/pallas_call | solution.py:103
  6.7 15.0 %all_to_all.25 = f32[32,8,128]{2,1,0:T(8,128)S(1)} all-to-all(f32[32,8,128]{2,1,0:T(8,128)S(1)} %get-tuple-element.15), channel_id=1, replica_groups=mesh['zh'=4,'zl'=2,'x'=4,'y'=4,'c'=2] {'x','y','c'}, dimensions={0} | all-to-all | bytes 262144 | tf_op jit(solution)/shard_map/all_to_all | solution.py:42
  21.7 13.5 %all_to_all.26 = f32[8,8,128]{2,1,0:T(8,128)S(1)} all-to-all(f32[8,8,128]{2,1,0:T(8,128)S(1)} %broadcast_in_dim.6), channel_id=1, replica_groups=mesh['zh'=4,'zl'=2,'x'=4,'y'=4,'c'=2] {'zh','zl'}, dimensions={0} | all-to-all | bytes 65536 | tf_op jit(solution)/shard_map/all_to_all | solution.py:38
  35.2 11.3 %all_to_all.27.tiles_ref = f32[32,8,128]{2,1,0:T(8,128)S(1)} all-to-all(f32[32,8,128]{2,1,0:T(8,128)S(1)} %broadcast_in_dim.7), channel_id=1, replica_groups=mesh['zh'=4,'zl'=2,'x'=4,'y'=4,'c'=2] {'x','y','c'}, dimensions={0} | all-to-all | bytes 262144 | tf_op jit(solution)/shard_map/all_to_all | solution.py:38
  46.4 4.9 %factor.1 = (f32[64,512]{1,0:T(8,128)}, bf16[64,512]{1,0:T(8,128)(2,1)S(1)}, f32[8,32,896]{2,1,0:T(8,128)S(1)}) custom-call(f32[32,8,128]{2,1,0:T(8,128)S(1)} %all_to_all.27.tiles_ref, bf16[4,512,896]{2,1,0:T(8,128)(2,1)} %get-tuple-element.16.corrected_hbm), custom_call_target="tpu_custom_call" | custom-call | tf_op jit(solution)/shard_map/factor/pallas_call | solution.py:204
  51.3 17.3 %all_to_all.28 = f32[8,32,896]{2,1,0:T(8,128)S(1)} all-to-all(f32[8,32,896]{2,1,0:T(8,128)S(1)} %get-tuple-element.18), channel_id=1, replica_groups=mesh['zh'=4,'zl'=2,'x'=4,'y'=4,'c'=2] {'zl','x'}, dimensions={0} | all-to-all | bytes 1835008 | tf_op jit(solution)/shard_map/all_to_all | solution.py:303
  68.7 2.6 %collective-permute-start.2 = (f32[32,896]{1,0:T(8,128)S(1)}, f32[32,896]{1,0:T(8,128)S(1)}, u32[]{:S(2)}, u32[]{:S(2)}) collective-permute-start(f32[32,896]{1,0:T(8,128)S(1)} %reduce_sum.29.after_ref), channel_id=1, source_target_pairs={{0,192},{64,0},{128,64},{192,128},{1,193},{65,1},{129,65},{193,129... | collective-permute-start | bytes 344072 | tf_op jit(solution)/shard_map/ppermute | solution.py:32
  71.2 1.6 %collective-permute-start.1 = (f32[32,896]{1,0:T(8,128)S(1)}, f32[32,896]{1,0:T(8,128)S(1)}, u32[]{:S(2)}, u32[]{:S(2)}) collective-permute-start(f32[32,896]{1,0:T(8,128)S(1)} %reduce_sum.29.after_ref), channel_id=1, source_target_pairs={{0,64},{64,128},{128,192},{192,0},{1,65},{65,129},{129,193},{193,1... | collective-permute-start | bytes 344072 | tf_op jit(solution)/shard_map/ppermute | solution.py:32
  72.9 2.9 %collective-permute-start = (f32[32,896]{1,0:T(8,128)S(1)}, f32[32,896]{1,0:T(8,128)S(1)}, u32[]{:S(2)}, u32[]{:S(2)}) collective-permute-start(f32[32,896]{1,0:T(8,128)S(1)} %reduce_sum.29.after_ref), channel_id=1, source_target_pairs={{0,128},{64,192},{128,0},{192,64},{1,129},{65,193},{129,1},{193,65... | collective-permute-start | bytes 344072 | tf_op jit(solution)/shard_map/ppermute | solution.py:32
  75.7 1.5 %fetch.1 = (bf16[512,64]{1,0:T(8,128)(2,1)S(1)}, bf16[2,512,896]{2,1,0:T(8,128)(2,1)S(1)}) custom-call(f32[32,896]{1,0:T(8,128)S(1)} %reduce_sum.29.after_ref, bf16[64,512]{1,0:T(8,128)(2,1)S(1)} %get-tuple-element.19.low_ref, bf16[4,512,896]{2,1,0:T(8,128)(2,1)} %get-tuple-element.16.corrected_hbm), custom_call_target="tpu_custom_call" | custom-call | tf_op jit(solution)/shard_map/fetch/pallas_call | solution.py:229
  77.3 1.6 %collective-permute-done.2 = f32[32,896]{1,0:T(8,128)S(1)} collective-permute-done((f32[32,896]{1,0:T(8,128)S(1)}, f32[32,896]{1,0:T(8,128)S(1)}, u32[]{:S(2)}, u32[]{:S(2)}) %collective-permute-start.2) | collective-permute-done | bytes 114720 | tf_op jit(solution)/shard_map/ppermute | solution.py:32
  78.8 1.1 %collective-permute-done.1 = f32[32,896]{1,0:T(8,128)S(1)} collective-permute-done((f32[32,896]{1,0:T(8,128)S(1)}, f32[32,896]{1,0:T(8,128)S(1)}, u32[]{:S(2)}, u32[]{:S(2)}) %collective-permute-start.1) | collective-permute-done | bytes 114720 | tf_op jit(solution)/shard_map/ppermute | solution.py:32
  79.9 4.1 %collective-permute-done = f32[32,896]{1,0:T(8,128)S(1)} collective-permute-done((f32[32,896]{1,0:T(8,128)S(1)}, f32[32,896]{1,0:T(8,128)S(1)}, u32[]{:S(2)}, u32[]{:S(2)}) %collective-permute-start) | collective-permute-done | bytes 114720 | tf_op jit(solution)/shard_map/ppermute | solution.py:32
  84.0 0.1 broadcast_in_dim.8
  84.1 16.5 %all_to_all.29.total_ref = f32[8,32,896]{2,1,0:T(8,128)S(1)} all-to-all(f32[8,32,896]{2,1,0:T(8,128)S(1)} %broadcast_in_dim.8), channel_id=1, replica_groups=mesh['zh'=4,'zl'=2,'x'=4,'y'=4,'c'=2] {'zl','x'}, dimensions={0} | all-to-all | bytes 1835008 | tf_op jit(solution)/shard_map/all_to_all | solution.py:38
  100.6 3.5 %feedback.1 = (f32[64,3584]{1,0:T(8,128)}, bf16[512,3584]{1,0:T(8,128)(2,1)}) custom-call(f32[8,32,896]{2,1,0:T(8,128)S(1)} %all_to_all.29.total_ref, bf16[512,64]{1,0:T(8,128)(2,1)S(1)} %get-tuple-element.23.low_t_ref, bf16[2,512,896]{2,1,0:T(8,128)(2,1)S(1)} %get-tuple-element.24.early_ref, bf16[4,512,896]{2,1,0:T(8,128)(2,1)} %get-tuple-element.16.corrected_hbm), custom_call_target="tpu_custom_call" | custom-call | tf_op jit(solution)/shard_map/feedback/pallas_call | solution.py:278
  (6 shorter events, 0.1 us)
Async XLA Ops:
  68.7 10.2 %collective-permute-start.2 = (f32[32,896]{1,0:T(8,128)S(1)}, f32[32,896]{1,0:T(8,128)S(1)}, u32[]{:S(2)}, u32[]{:S(2)}) collective-permute-start(f32[32,896]{1,0:T(8,128)S(1)} %reduce_sum.29.after_ref), channel_id=1, source_target_pairs={{0,192},{64,0},{128,64},{192,128},{1,193},{65,1},{129,65},{193,129... | collective-permute-start | bytes 344072 | tf_op jit(solution)/shard_map/ppermute | solution.py:32
  71.2 8.7 %collective-permute-start.1 = (f32[32,896]{1,0:T(8,128)S(1)}, f32[32,896]{1,0:T(8,128)S(1)}, u32[]{:S(2)}, u32[]{:S(2)}) collective-permute-start(f32[32,896]{1,0:T(8,128)S(1)} %reduce_sum.29.after_ref), channel_id=1, source_target_pairs={{0,64},{64,128},{128,192},{192,0},{1,65},{65,129},{129,193},{193,1... | collective-permute-start | bytes 344072 | tf_op jit(solution)/shard_map/ppermute | solution.py:32
  72.9 11.2 %collective-permute-start = (f32[32,896]{1,0:T(8,128)S(1)}, f32[32,896]{1,0:T(8,128)S(1)}, u32[]{:S(2)}, u32[]{:S(2)}) collective-permute-start(f32[32,896]{1,0:T(8,128)S(1)} %reduce_sum.29.after_ref), channel_id=1, source_target_pairs={{0,128},{64,192},{128,0},{192,64},{1,129},{65,193},{129,1},{193,65... | collective-permute-start | bytes 344072 | tf_op jit(solution)/shard_map/ppermute | solution.py:32

commit v5 on v4

--- a/solution.py
+++ b/solution.py
@@ -15,6 +15,7 @@
 REPLICAS = SIZES["zh"] * SIZES["zl"] * SIZES["x"]
 QUARTERS = SIZES["x"]
 HALVES = SIZES["zl"]
+AHEAD = 2
 EARLY = 2
 VMEM = pltpu.CompilerParams(vmem_limit_bytes=20 << 20)
 
@@ -45,8 +46,8 @@
 
 
 def corrected_kernel(
-    x_hbm, g_hbm, fb_hbm, basis_hbm, corrected_hbm, tiles_ref,
-    x_ref, g_ref, fb_ref, basis_ref, out_ref, x_sem, in_sems, out_sems,
+    x_hbm, g_hbm, fb_hbm, basis_hbm, early_ref, late_hbm, tiles_ref,
+    x_ref, g_ref, fb_ref, basis_ref, late_ref, x_sem, in_sems, out_sems,
 ):
     width = g_ref.shape[2]
     fetch_x = pltpu.make_async_copy(x_hbm, x_ref, x_sem)
@@ -61,15 +62,17 @@
                 for i, (whole, part) in enumerate(pairs)
             ]
         )
+    for q in range(AHEAD):
         for fetch in fetches[q]:
             fetch.start()
     fetch_x.wait()
     xt = x_ref[...].T
+    corrected = lambda q: early_ref.at[q] if q < EARLY else late_ref.at[q - EARLY]
 
     def factor_part(q):
         return lax.dot_general(
             basis_ref[q].astype(jnp.bfloat16),
-            out_ref[q],
+            corrected(q)[...],
             (((1,), (1,)), ((), ())),
             preferred_element_type=jnp.float32,
         )
@@ -79,13 +82,18 @@
     for q in range(QUARTERS):
         for fetch in fetches[q]:
             fetch.wait()
+        if q + AHEAD < QUARTERS:
+            for fetch in fetches[q + AHEAD]:
+                fetch.start()
         grad = jnp.dot(xt, g_ref[q], preferred_element_type=jnp.float32)
         if q:
             parts.append(factor_part(q - 1))
         grad = grad * (1.0 / math.sqrt(x_ref.shape[0])) + fb_ref[q].astype(jnp.float32)
-        out_ref[q] = grad.astype(jnp.bfloat16)
-        stores.append(pltpu.make_async_copy(out_ref.at[q], corrected_hbm.at[q], out_sems.at[q]))
-        stores[q].start()
+        corrected(q)[...] = grad.astype(jnp.bfloat16)
+        if q >= EARLY:
+            late = q - EARLY
+            stores.append(pltpu.make_async_copy(late_ref.at[late], late_hbm.at[late], out_sems.at[late]))
+            stores[-1].start()
     parts.append(factor_part(QUARTERS - 1))
     total = sum(parts[1:], parts[0])
     rows, columns = total.shape
@@ -103,9 +111,10 @@
     return pl.pallas_call(
         corrected_kernel,
         in_specs=[pl.BlockSpec(memory_space=pltpu.HBM)] * 4,
-        out_specs=[pl.BlockSpec(memory_space=pltpu.HBM), pl.BlockSpec(memory_space=pltpu.VMEM)],
+        out_specs=[pl.BlockSpec(memory_space=space) for space in (pltpu.VMEM, pltpu.HBM, pltpu.VMEM)],
         out_shape=[
-            pltpu.HBM((QUARTERS, rows, width), jnp.bfloat16),
+            pltpu.VMEM((EARLY, rows, width), jnp.bfloat16),
+            pltpu.HBM((QUARTERS - EARLY, rows, width), jnp.bfloat16),
             jax.ShapeDtypeStruct((rank * rows // 1024, 8, 128), jnp.float32),
         ],
         scratch_shapes=[
@@ -113,10 +122,10 @@
             pltpu.VMEM((QUARTERS, tokens, width), jnp.bfloat16),
             pltpu.VMEM((QUARTERS, rows, width), jnp.bfloat16),
             pltpu.VMEM((QUARTERS, rank, width), jnp.float32),
-            pltpu.VMEM((QUARTERS, rows, width), jnp.bfloat16),
+            pltpu.VMEM((QUARTERS - EARLY, rows, width), jnp.bfloat16),
             pltpu.SemaphoreType.DMA(()),
             pltpu.SemaphoreType.DMA((QUARTERS, 3)),
-            pltpu.SemaphoreType.DMA((QUARTERS,)),
+            pltpu.SemaphoreType.DMA((QUARTERS - EARLY,)),
         ],
         compiler_params=VMEM,
         name="corrected",
@@ -173,8 +182,8 @@
     return out
 
 
-def factor_kernel(tiles_ref, corrected_hbm, left_ref, low_ref, terms_ref, corrected_ref, sem):
-    fetch = pltpu.make_async_copy(corrected_hbm, corrected_ref, sem)
+def factor_kernel(tiles_ref, early_ref, late_hbm, left_ref, low_ref, terms_ref, late_ref, sem):
+    fetch = pltpu.make_async_copy(late_hbm, late_ref, sem)
     fetch.start()
     rank, columns = left_ref.shape
     lanes = columns // 128
@@ -191,62 +200,55 @@
             left_ref[8 * i : 8 * i + 8, 128 * j : 128 * j + 128] = tile
     low = left_ref[...].astype(jnp.bfloat16)
     low_ref[...] = low
-    fetch.wait()
     for q in range(QUARTERS):
-        term = jnp.dot(low, corrected_ref[q], preferred_element_type=jnp.float32)
+        if q == EARLY:
+            fetch.wait()
+        corrected = early_ref[q] if q < EARLY else late_ref[q - EARLY]
+        term = jnp.dot(low, corrected, preferred_element_type=jnp.float32)
         for h in range(HALVES):
             terms_ref[h * QUARTERS + q] = term[h * (rank // HALVES) : (h + 1) * (rank // HALVES)]
 
 
-def factor_and_terms(tiles, corrected, rank):
-    quarters, rows, width = corrected.shape
+def factor_and_terms(tiles, early, late, rank):
+    _, rows, width = late.shape
     whole = pl.BlockSpec(memory_space=pltpu.VMEM)
     return pl.pallas_call(
         factor_kernel,
-        in_specs=[whole, pl.BlockSpec(memory_space=pltpu.HBM)],
+        in_specs=[whole, whole, pl.BlockSpec(memory_space=pltpu.HBM)],
         out_specs=[whole] * 3,
         out_shape=[
             jax.ShapeDtypeStruct((rank, rows), jnp.float32),
             jax.ShapeDtypeStruct((rank, rows), jnp.bfloat16),
-            jax.ShapeDtypeStruct((HALVES * quarters, rank // HALVES, width), jnp.float32),
-        ],
-        scratch_shapes=[pltpu.VMEM(corrected.shape, jnp.bfloat16), pltpu.SemaphoreType.DMA(())],
+            jax.ShapeDtypeStruct((HALVES * QUARTERS, rank // HALVES, width), jnp.float32),
+        ],
+        scratch_shapes=[pltpu.VMEM(late.shape, jnp.bfloat16), pltpu.SemaphoreType.DMA(())],
         compiler_params=VMEM,
         name="factor",
-    )(tiles, *in_hbm(corrected))
-
-
-def fetch_kernel(after_ref, low_ref, corrected_hbm, low_t_ref, fetched_ref, sem):
-    fetch = pltpu.make_async_copy(corrected_hbm.at[pl.ds(0, EARLY)], fetched_ref, sem)
-    fetch.start()
+    )(tiles, *in_vmem(early), *in_hbm(late))
+
+
+def transpose_kernel(after_ref, low_ref, low_t_ref):
     low_t_ref[...] = low_ref[...].astype(jnp.float32).T.astype(jnp.bfloat16)
-    fetch.wait()
-
-
-def fetch_after(before, low, corrected):
-    rank, rows = low.shape
-    whole = pl.BlockSpec(memory_space=pltpu.VMEM)
+
+
+def transposed_after(before, low):
     return pl.pallas_call(
-        fetch_kernel,
-        in_specs=[pl.BlockSpec(memory_space=pl.ANY), whole, pl.BlockSpec(memory_space=pltpu.HBM)],
-        out_specs=[whole, whole],
-        out_shape=[
-            pltpu.VMEM((rows, rank), low.dtype),
-            pltpu.VMEM((EARLY,) + corrected.shape[1:], corrected.dtype),
-        ],
-        scratch_shapes=[pltpu.SemaphoreType.DMA(())],
+        transpose_kernel,
+        in_specs=[pl.BlockSpec(memory_space=pl.ANY), pl.BlockSpec(memory_space=pltpu.VMEM)],
+        out_specs=pl.BlockSpec(memory_space=pltpu.VMEM),
+        out_shape=pltpu.VMEM(low.shape[::-1], low.dtype),
         compiler_params=VMEM,
-        name="fetch",
-    )(before, low, *in_hbm(corrected))
+        name="transpose",
+    )(before, low)
 
 
 def feedback_kernel(
-    total_ref, low_t_ref, early_ref, corrected_hbm, next_hbm, feedback_hbm, next_ref, out_ref, late_ref, sems, late_sems
+    total_ref, low_t_ref, early_ref, late_hbm, next_hbm, feedback_hbm, next_ref, out_ref, late_ref, sems, late_sems
 ):
     quarters, rows, width = out_ref.shape
     fetches = [
-        pltpu.make_async_copy(corrected_hbm.at[q], late_ref.at[q - EARLY], late_sems.at[q - EARLY])
-        for q in range(EARLY, quarters)
+        pltpu.make_async_copy(late_hbm.at[i], late_ref.at[i], late_sems.at[i])
+        for i in range(late_ref.shape[0])
     ]
     for fetch in fetches:
         fetch.start()
@@ -270,8 +272,9 @@
         store.wait()
 
 
-def finish(total, low_t, early, corrected):
-    quarters, rows, width = corrected.shape
+def finish(total, low_t, early, late):
+    _, rows, width = late.shape
+    quarters = QUARTERS
     rank = low_t.shape[1]
     hbm = pl.BlockSpec(memory_space=pltpu.HBM)
     whole = pl.BlockSpec(memory_space=pltpu.VMEM)
@@ -292,20 +295,20 @@
         ],
         compiler_params=VMEM,
         name="feedback",
-    )(total, *in_vmem(low_t, early), *in_hbm(corrected))
+    )(total, *in_vmem(low_t, early), *in_hbm(late))
 
 
 def local(layer_input, output_grad, feedback, basis_prev):
-    corrected, tiles = corrected_and_factor(layer_input, output_grad, feedback, basis_prev)
+    early, late, tiles = corrected_and_factor(layer_input, output_grad, feedback, basis_prev)
     tiles = sum_all(tiles)
-    factor_left, factor_low, terms = factor_and_terms(tiles, corrected, basis_prev.shape[0])
+    factor_left, factor_low, terms = factor_and_terms(tiles, early, late, basis_prev.shape[0])
 
     block = jnp.sum(lax.all_to_all(terms, NEAR, 0, 0, tiled=True), 0)
     one, two, three = (shift(block, "zh", k) for k in (1, 2, 3))
-    low_t, early = fetch_after(block, factor_low, corrected)
+    low_t = transposed_after(block, factor_low)
     block = (block + two) + (one + three)
-    block, low_t, early = lax.optimization_barrier((block, low_t, early))
-    basis_next, feedback_next = finish(copies(block, NEAR), low_t, early, corrected)
+    block, low_t = lax.optimization_barrier((block, low_t))
+    basis_next, feedback_next = finish(copies(block, NEAR), low_t, early, late)
     return factor_left, basis_next, feedback_next
 
 

time: 105 us -> 103 us (0.981)
  Pallas kernels: 15.9 us -> 13.1 us
  waiting for transfers between devices: 6.76 us -> 8.17 us
    pallas_call x2, Pallas kernels: 6.41 us -> 4.24 us  [the longest x1 4.14 us: factor_and_terms(): pl.pallas_call(factor_kernel, in_specs=[whole, whole, pl.BlockSpec(memory...]
    ppermute x3, waiting for transfers between devices: 6.76 us -> 8.17 us  [shift(): return lax.ppermute(block, axis, [(i, (i + step) % n) for i in range(n)])]
  transfers between devices with their start and end apart: 3 -> 3, of which waited for: 3 -> 3; matrix products, arithmetic and copies ran while one was open for 0% -> 0% of each run, Pallas kernels for 1% -> 0%
where the time goes in v5:
time: 103 us
  blocking collectives  73.5 us (71%)
  Pallas kernels  13.1 us (13%)
  waiting for transfers between devices  8.17 us (8%)
  starting transfers between devices  7.08 us (7%)
    all_to_all x3, blocking collectives, copies(): return lax.all_to_all(sent, axes, 0, 0, tiled=True)  41.2 us
    all_to_all x1, blocking collectives, local(): block = jnp.sum(lax.all_to_all(terms, NEAR, 0, 0, tiled=True), 0)  17.3 us
    all_to_all x1, blocking collectives, sum_all(): parts = lax.all_to_all(tiles, PLANE, 0, 0, tiled=True)  15 us
    ppermute x3, waiting for transfers between devices, shift(): return lax.ppermute(block, axis, [(i, (i + step) % n) for i in range(n)])  8.17 us
    ppermute x3, starting transfers between devices, shift(): return lax.ppermute(block, axis, [(i, (i + step) % n) for i in range(n)])  7.08 us
    pallas_call x1, Pallas kernels, corrected_and_factor(): pl.pallas_call(corrected_kernel, in_specs=[pl.BlockSpec(memory_space=pltp...  5.51 us
    pallas_call x1, Pallas kernels, factor_and_terms(): pl.pallas_call(factor_kernel, in_specs=[whole, whole, pl.BlockSpec(memory...  4.14 us
    pallas_call x1, Pallas kernels, finish(): pl.pallas_call(feedback_kernel, in_specs=[whole, whole, whole, hbm], out_...  3.33 us
  transfers between devices with their start and end apart: 3, of which 3 were waited for; matrix products, arithmetic and copies ran while one was open for 0% of the time, Pallas kernels for 0%

profile of v5, /device:TPU:64, one launch (start us, length us, event | category | flops | bytes accessed | tf_op | source)
XLA Modules:
  0.0 102.7 jit_solution(13514743362070145827)
XLA Ops:
  0.6 5.5 %corrected.1 = (bf16[2,512,896]{2,1,0:T(8,128)(2,1)S(1)}, bf16[2,512,896]{2,1,0:T(8,128)(2,1)}, f32[32,8,128]{2,1,0:T(8,128)S(1)}) custom-call(bf16[256,512]{1,0:T(8,128)(2,1)} %x_hbm.1, bf16[256,3584]{1,0:T(8,128)(2,1)} %g_hbm.1, bf16[512,3584]{1,0:T(8,128)(2,1)} %fb_hbm.1, f32[64,3584]{1,0:T(8,128)} %basis_hbm.1), custom_call_target="tpu_custom_call" | custom-call | tf_op jit(solution)/shard_map/corrected/pallas_call | solution.py:111
  6.1 15.0 %all_to_all.25 = f32[32,8,128]{2,1,0:T(8,128)S(1)} all-to-all(f32[32,8,128]{2,1,0:T(8,128)S(1)} %get-tuple-element.13), channel_id=1, replica_groups=mesh['zh'=4,'zl'=2,'x'=4,'y'=4,'c'=2] {'x','y','c'}, dimensions={0} | all-to-all | bytes 262144 | tf_op jit(solution)/shard_map/all_to_all | solution.py:43
  21.2 13.4 %all_to_all.26 = f32[8,8,128]{2,1,0:T(8,128)S(1)} all-to-all(f32[8,8,128]{2,1,0:T(8,128)S(1)} %broadcast_in_dim.6), channel_id=1, replica_groups=mesh['zh'=4,'zl'=2,'x'=4,'y'=4,'c'=2] {'zh','zl'}, dimensions={0} | all-to-all | bytes 65536 | tf_op jit(solution)/shard_map/all_to_all | solution.py:39
  34.6 11.3 %all_to_all.27.tiles_ref = f32[32,8,128]{2,1,0:T(8,128)S(1)} all-to-all(f32[32,8,128]{2,1,0:T(8,128)S(1)} %broadcast_in_dim.7), channel_id=1, replica_groups=mesh['zh'=4,'zl'=2,'x'=4,'y'=4,'c'=2] {'x','y','c'}, dimensions={0} | all-to-all | bytes 262144 | tf_op jit(solution)/shard_map/all_to_all | solution.py:39
  45.9 4.1 %factor.1 = (f32[64,512]{1,0:T(8,128)}, bf16[64,512]{1,0:T(8,128)(2,1)S(1)}, f32[8,32,896]{2,1,0:T(8,128)S(1)}) custom-call(f32[32,8,128]{2,1,0:T(8,128)S(1)} %all_to_all.27.tiles_ref, bf16[2,512,896]{2,1,0:T(8,128)(2,1)S(1)} %get-tuple-element.14.early_ref, bf16[2,512,896]{2,1,0:T(8,128)(2,1)} %get-tuple-element.15.late_hbm), custom_call_target="tpu_custom_call" | custom-call | tf_op jit(solution)/shard_map/factor/pallas_call | solution.py:215
  50.1 17.3 %all_to_all.28 = f32[8,32,896]{2,1,0:T(8,128)S(1)} all-to-all(f32[8,32,896]{2,1,0:T(8,128)S(1)} %get-tuple-element.17), channel_id=1, replica_groups=mesh['zh'=4,'zl'=2,'x'=4,'y'=4,'c'=2] {'zl','x'}, dimensions={0} | all-to-all | bytes 1835008 | tf_op jit(solution)/shard_map/all_to_all | solution.py:306
  67.4 2.6 %collective-permute-start.2 = (f32[32,896]{1,0:T(8,128)S(1)}, f32[32,896]{1,0:T(8,128)S(1)}, u32[]{:S(2)}, u32[]{:S(2)}) collective-permute-start(f32[32,896]{1,0:T(8,128)S(1)} %reduce_sum.29.after_ref), channel_id=1, source_target_pairs={{0,192},{64,0},{128,64},{192,128},{1,193},{65,1},{129,65},{193,129... | collective-permute-start | bytes 344072 | tf_op jit(solution)/shard_map/ppermute | solution.py:33
  69.9 1.6 %collective-permute-start.1 = (f32[32,896]{1,0:T(8,128)S(1)}, f32[32,896]{1,0:T(8,128)S(1)}, u32[]{:S(2)}, u32[]{:S(2)}) collective-permute-start(f32[32,896]{1,0:T(8,128)S(1)} %reduce_sum.29.after_ref), channel_id=1, source_target_pairs={{0,64},{64,128},{128,192},{192,0},{1,65},{65,129},{129,193},{193,1... | collective-permute-start | bytes 344072 | tf_op jit(solution)/shard_map/ppermute | solution.py:33
  71.6 2.9 %collective-permute-start = (f32[32,896]{1,0:T(8,128)S(1)}, f32[32,896]{1,0:T(8,128)S(1)}, u32[]{:S(2)}, u32[]{:S(2)}) collective-permute-start(f32[32,896]{1,0:T(8,128)S(1)} %reduce_sum.29.after_ref), channel_id=1, source_target_pairs={{0,128},{64,192},{128,0},{192,64},{1,129},{65,193},{129,1},{193,65... | collective-permute-start | bytes 344072 | tf_op jit(solution)/shard_map/ppermute | solution.py:33
  74.5 0.1 transpose.4.low_t_ref
  74.6 3.0 %collective-permute-done.2 = f32[32,896]{1,0:T(8,128)S(1)} collective-permute-done((f32[32,896]{1,0:T(8,128)S(1)}, f32[32,896]{1,0:T(8,128)S(1)}, u32[]{:S(2)}, u32[]{:S(2)}) %collective-permute-start.2) | collective-permute-done | bytes 114720 | tf_op jit(solution)/shard_map/ppermute | solution.py:33
  77.5 1.1 %collective-permute-done.1 = f32[32,896]{1,0:T(8,128)S(1)} collective-permute-done((f32[32,896]{1,0:T(8,128)S(1)}, f32[32,896]{1,0:T(8,128)S(1)}, u32[]{:S(2)}, u32[]{:S(2)}) %collective-permute-start.1) | collective-permute-done | bytes 114720 | tf_op jit(solution)/shard_map/ppermute | solution.py:33
  78.6 4.1 %collective-permute-done = f32[32,896]{1,0:T(8,128)S(1)} collective-permute-done((f32[32,896]{1,0:T(8,128)S(1)}, f32[32,896]{1,0:T(8,128)S(1)}, u32[]{:S(2)}, u32[]{:S(2)}) %collective-permute-start) | collective-permute-done | bytes 114720 | tf_op jit(solution)/shard_map/ppermute | solution.py:33
  82.8 0.1 broadcast_in_dim.8
  82.8 16.5 %all_to_all.29.total_ref = f32[8,32,896]{2,1,0:T(8,128)S(1)} all-to-all(f32[8,32,896]{2,1,0:T(8,128)S(1)} %broadcast_in_dim.8), channel_id=1, replica_groups=mesh['zh'=4,'zl'=2,'x'=4,'y'=4,'c'=2] {'zl','x'}, dimensions={0} | all-to-all | bytes 1835008 | tf_op jit(solution)/shard_map/all_to_all | solution.py:39
  99.3 3.3 %feedback.1 = (f32[64,3584]{1,0:T(8,128)}, bf16[512,3584]{1,0:T(8,128)(2,1)}) custom-call(f32[8,32,896]{2,1,0:T(8,128)S(1)} %all_to_all.29.total_ref, bf16[512,64]{1,0:T(8,128)(2,1)S(1)} %transpose.4.low_t_ref, bf16[2,512,896]{2,1,0:T(8,128)(2,1)S(1)} %get-tuple-element.14.early_ref, bf16[2,512,896]{2,1,0:T(8,128)(2,1)} %get-tuple-element.15.late_hbm), custom_call_target="tpu_custom_call" | custom-call | tf_op jit(solution)/shard_map/feedback/pallas_call | solution.py:281
  (6 shorter events, 0.1 us)
Async XLA Ops:
  67.4 10.2 %collective-permute-start.2 = (f32[32,896]{1,0:T(8,128)S(1)}, f32[32,896]{1,0:T(8,128)S(1)}, u32[]{:S(2)}, u32[]{:S(2)}) collective-permute-start(f32[32,896]{1,0:T(8,128)S(1)} %reduce_sum.29.after_ref), channel_id=1, source_target_pairs={{0,192},{64,0},{128,64},{192,128},{1,193},{65,1},{129,65},{193,129... | collective-permute-start | bytes 344072 | tf_op jit(solution)/shard_map/ppermute | solution.py:33
  69.9 8.7 %collective-permute-start.1 = (f32[32,896]{1,0:T(8,128)S(1)}, f32[32,896]{1,0:T(8,128)S(1)}, u32[]{:S(2)}, u32[]{:S(2)}) collective-permute-start(f32[32,896]{1,0:T(8,128)S(1)} %reduce_sum.29.after_ref), channel_id=1, source_target_pairs={{0,64},{64,128},{128,192},{192,0},{1,65},{65,129},{129,193},{193,1... | collective-permute-start | bytes 344072 | tf_op jit(solution)/shard_map/ppermute | solution.py:33
  71.6 11.2 %collective-permute-start = (f32[32,896]{1,0:T(8,128)S(1)}, f32[32,896]{1,0:T(8,128)S(1)}, u32[]{:S(2)}, u32[]{:S(2)}) collective-permute-start(f32[32,896]{1,0:T(8,128)S(1)} %reduce_sum.29.after_ref), channel_id=1, source_target_pairs={{0,128},{64,192},{128,0},{192,64},{1,129},{65,193},{129,1},{193,65... | collective-permute-start | bytes 344072 | tf_op jit(solution)/shard_map/ppermute | solution.py:33

commit v6 on v5

--- a/solution.py
+++ b/solution.py
@@ -9,13 +9,13 @@
 from jax.sharding import PartitionSpec as P
 
 SIZES = dict(zh=4, zl=2, x=4, y=4, c=2)
-PLANE = ("x", "y", "c")
-LINE = ("zh", "zl")
+FIRST = ("zl", "x", "c")
+REST = ("zh", "y")
 NEAR = ("zl", "x")
 REPLICAS = SIZES["zh"] * SIZES["zl"] * SIZES["x"]
 QUARTERS = SIZES["x"]
 HALVES = SIZES["zl"]
-AHEAD = 2
+SPANS = 2
 EARLY = 2
 VMEM = pltpu.CompilerParams(vmem_limit_bytes=20 << 20)
 
@@ -40,61 +40,61 @@
 
 
 def sum_all(tiles):
-    parts = lax.all_to_all(tiles, PLANE, 0, 0, tiled=True)
-    parts = copies(jnp.sum(parts, 0), LINE)
-    return copies(jnp.sum(parts, 0), PLANE)
+    members = math.prod(SIZES[a] for a in FIRST)
+    parts = lax.all_to_all(tiles, FIRST, 0, 0, tiled=True)
+    piece = jnp.sum(parts.reshape((members, -1) + tiles.shape[1:]), 0)
+    piece = jnp.sum(copies(piece, REST), 0)
+    return copies(piece, FIRST).reshape(tiles.shape)
 
 
 def corrected_kernel(
     x_hbm, g_hbm, fb_hbm, basis_hbm, early_ref, late_hbm, tiles_ref,
     x_ref, g_ref, fb_ref, basis_ref, late_ref, x_sem, in_sems, out_sems,
 ):
-    width = g_ref.shape[2]
+    span = g_ref.shape[2]
+    width = early_ref.shape[2]
     fetch_x = pltpu.make_async_copy(x_hbm, x_ref, x_sem)
     fetch_x.start()
     fetches = []
-    for q in range(QUARTERS):
-        columns = pl.ds(q * width, width)
+    for n in range(SPANS):
+        columns = pl.ds(n * span, span)
         pairs = ((g_hbm, g_ref), (fb_hbm, fb_ref), (basis_hbm, basis_ref))
         fetches.append(
             [
-                pltpu.make_async_copy(whole.at[:, columns], part.at[q], in_sems.at[q, i])
+                pltpu.make_async_copy(whole.at[:, columns], part.at[n], in_sems.at[n, i])
                 for i, (whole, part) in enumerate(pairs)
             ]
         )
-    for q in range(AHEAD):
-        for fetch in fetches[q]:
+        for fetch in fetches[n]:
             fetch.start()
     fetch_x.wait()
     xt = x_ref[...].T
-    corrected = lambda q: early_ref.at[q] if q < EARLY else late_ref.at[q - EARLY]
-
-    def factor_part(q):
-        return lax.dot_general(
-            basis_ref[q].astype(jnp.bfloat16),
-            corrected(q)[...],
-            (((1,), (1,)), ((), ())),
-            preferred_element_type=jnp.float32,
-        )
-
     parts = []
     stores = []
-    for q in range(QUARTERS):
-        for fetch in fetches[q]:
+    for n in range(SPANS):
+        for fetch in fetches[n]:
             fetch.wait()
-        if q + AHEAD < QUARTERS:
-            for fetch in fetches[q + AHEAD]:
-                fetch.start()
-        grad = jnp.dot(xt, g_ref[q], preferred_element_type=jnp.float32)
-        if q:
-            parts.append(factor_part(q - 1))
-        grad = grad * (1.0 / math.sqrt(x_ref.shape[0])) + fb_ref[q].astype(jnp.float32)
-        corrected(q)[...] = grad.astype(jnp.bfloat16)
-        if q >= EARLY:
-            late = q - EARLY
-            stores.append(pltpu.make_async_copy(late_ref.at[late], late_hbm.at[late], out_sems.at[late]))
-            stores[-1].start()
-    parts.append(factor_part(QUARTERS - 1))
+        grad = jnp.dot(xt, g_ref[n], preferred_element_type=jnp.float32)
+        grad = grad * (1.0 / math.sqrt(x_ref.shape[0])) + fb_ref[n].astype(jnp.float32)
+        corrected = grad.astype(jnp.bfloat16)
+        for i in range(span // width):
+            q = n * (span // width) + i
+            piece = corrected[:, i * width : (i + 1) * width]
+            if q < EARLY:
+                early_ref[q] = piece
+            else:
+                late = q - EARLY
+                late_ref[late] = piece
+                stores.append(pltpu.make_async_copy(late_ref.at[late], late_hbm.at[late], out_sems.at[late]))
+                stores[-1].start()
+        parts.append(
+            lax.dot_general(
+                basis_ref[n].astype(jnp.bfloat16),
+                corrected,
+                (((1,), (1,)), ((), ())),
+                preferred_element_type=jnp.float32,
+            )
+        )
     total = sum(parts[1:], parts[0])
     rows, columns = total.shape
     for i in range(rows // 8):
@@ -119,12 +119,12 @@
         ],
         scratch_shapes=[
             pltpu.VMEM((tokens, rows), jnp.bfloat16),
-            pltpu.VMEM((QUARTERS, tokens, width), jnp.bfloat16),
-            pltpu.VMEM((QUARTERS, rows, width), jnp.bfloat16),
-            pltpu.VMEM((QUARTERS, rank, width), jnp.float32),
+            pltpu.VMEM((SPANS, tokens, columns // SPANS), jnp.bfloat16),
+            pltpu.VMEM((SPANS, rows, columns // SPANS), jnp.bfloat16),
+            pltpu.VMEM((SPANS, rank, columns // SPANS), jnp.float32),
             pltpu.VMEM((QUARTERS - EARLY, rows, width), jnp.bfloat16),
             pltpu.SemaphoreType.DMA(()),
-            pltpu.SemaphoreType.DMA((QUARTERS, 3)),
+            pltpu.SemaphoreType.DMA((SPANS, 3)),
             pltpu.SemaphoreType.DMA((QUARTERS - EARLY,)),
         ],
         compiler_params=VMEM,

time: 103 us -> 103 us (level)
  blocking collectives: 73.5 us -> 74.6 us
    all_to_all x3, blocking collectives: 41.2 us -> 45.4 us  [copies(): return lax.all_to_all(sent, axes, 0, 0, tiled=True)]
    all_to_all x1, blocking collectives: 15 us -> 12.3 us  [sum_all(): parts = lax.all_to_all(tiles, FIRST, 0, 0, tiled=True)]
where the time goes in v6:
time: 103 us; the launch traced here: 102 us
  blocking collectives  74.6 us (72%)
  Pallas kernels  13 us (13%)
  waiting for transfers between devices  7.23 us (7%)
  starting transfers between devices  6.64 us (6%)
    all_to_all x3, blocking collectives, copies(): return lax.all_to_all(sent, axes, 0, 0, tiled=True)  45.4 us
    all_to_all x1, blocking collectives, local(): block = jnp.sum(lax.all_to_all(terms, NEAR, 0, 0, tiled=True), 0)  17 us
    all_to_all x1, blocking collectives, sum_all(): parts = lax.all_to_all(tiles, FIRST, 0, 0, tiled=True)  12.3 us
    ppermute x3, waiting for transfers between devices, shift(): return lax.ppermute(block, axis, [(i, (i + step) % n) for i in range(n)])  7.23 us
    ppermute x3, starting transfers between devices, shift(): return lax.ppermute(block, axis, [(i, (i + step) % n) for i in range(n)])  6.64 us
    pallas_call x1, Pallas kernels, corrected_and_factor(): pl.pallas_call(corrected_kernel, in_specs=[pl.BlockSpec(memory_space=pltp...  5.43 us
    pallas_call x1, Pallas kernels, factor_and_terms(): pl.pallas_call(factor_kernel, in_specs=[whole, whole, pl.BlockSpec(memory...  4.14 us
    pallas_call x1, Pallas kernels, finish(): pl.pallas_call(feedback_kernel, in_specs=[whole, whole, whole, hbm], out_...  3.33 us
  transfers between devices with their start and end apart: 3, of which 3 were waited for; matrix products, arithmetic and copies ran while one was open for 0% of the time, Pallas kernels for 0%

profile of v6, /device:TPU:64, one launch (start us, length us, event | category | flops | bytes accessed | tf_op | source)
XLA Modules:
  0.0 102.4 jit_solution(18090559917263924487)
XLA Ops:
  0.6 5.4 %corrected.1 = (bf16[2,512,896]{2,1,0:T(8,128)(2,1)S(1)}, bf16[2,512,896]{2,1,0:T(8,128)(2,1)}, f32[32,8,128]{2,1,0:T(8,128)S(1)}) custom-call(bf16[256,512]{1,0:T(8,128)(2,1)} %x_hbm.1, bf16[256,3584]{1,0:T(8,128)(2,1)} %g_hbm.1, bf16[512,3584]{1,0:T(8,128)(2,1)} %fb_hbm.1, f32[64,3584]{1,0:T(8,128)} %basis_hbm.1), custom_call_target="tpu_custom_call" | custom-call | tf_op jit(solution)/shard_map/corrected/pallas_call | solution.py:111
  6.1 12.3 %all_to_all.25 = f32[32,8,128]{2,1,0:T(8,128)S(1)} all-to-all(f32[32,8,128]{2,1,0:T(8,128)S(1)} %get-tuple-element.13), channel_id=1, replica_groups=mesh['zh'=4,'zl'=2,'x'=4,'y'=4,'c'=2] {'zl','x','c'}, dimensions={0} | all-to-all | bytes 262144 | tf_op jit(solution)/shard_map/all_to_all | solution.py:44
  18.4 18.0 %all_to_all.26 = f32[16,2,8,128]{3,2,1,0:T(8,128)S(1)} all-to-all(f32[16,2,8,128]{3,2,1,0:T(8,128)S(1)} %broadcast_in_dim.6), channel_id=1, replica_groups=mesh['zh'=4,'zl'=2,'x'=4,'y'=4,'c'=2] {'zh','y'}, dimensions={0} | all-to-all | bytes 262144 | tf_op jit(solution)/shard_map/all_to_all | solution.py:39
  36.4 9.7 %all_to_all.27 = f32[16,2,8,128]{3,2,1,0:T(8,128)S(1)} all-to-all(f32[16,2,8,128]{3,2,1,0:T(8,128)S(1)} %broadcast_in_dim.7), channel_id=1, replica_groups=mesh['zh'=4,'zl'=2,'x'=4,'y'=4,'c'=2] {'zl','x','c'}, dimensions={0} | all-to-all | bytes 262144 | tf_op jit(solution)/shard_map/all_to_all | solution.py:39
  46.1 4.1 %factor.1 = (f32[64,512]{1,0:T(8,128)}, bf16[64,512]{1,0:T(8,128)(2,1)S(1)}, f32[8,32,896]{2,1,0:T(8,128)S(1)}) custom-call(f32[32,8,128]{2,1,0:T(8,128)S(1)} %bitcast.2, bf16[2,512,896]{2,1,0:T(8,128)(2,1)S(1)} %get-tuple-element.14.early_ref, bf16[2,512,896]{2,1,0:T(8,128)(2,1)} %get-tuple-element.15.late_hbm), custom_call_target="tpu_custom_call" | custom-call | tf_op jit(solution)/shard_map/factor/pallas_call | solution.py:215
  50.2 17.0 %all_to_all.28 = f32[8,32,896]{2,1,0:T(8,128)S(1)} all-to-all(f32[8,32,896]{2,1,0:T(8,128)S(1)} %get-tuple-element.17), channel_id=1, replica_groups=mesh['zh'=4,'zl'=2,'x'=4,'y'=4,'c'=2] {'zl','x'}, dimensions={0} | all-to-all | bytes 1835008 | tf_op jit(solution)/shard_map/all_to_all | solution.py:306
  67.3 2.0 %collective-permute-start.2 = (f32[32,896]{1,0:T(8,128)S(1)}, f32[32,896]{1,0:T(8,128)S(1)}, u32[]{:S(2)}, u32[]{:S(2)}) collective-permute-start(f32[32,896]{1,0:T(8,128)S(1)} %reduce_sum.29.after_ref), channel_id=1, source_target_pairs={{0,192},{64,0},{128,64},{192,128},{1,193},{65,1},{129,65},{193,129... | collective-permute-start | bytes 344072 | tf_op jit(solution)/shard_map/ppermute | solution.py:33
  69.2 2.2 %collective-permute-start.1 = (f32[32,896]{1,0:T(8,128)S(1)}, f32[32,896]{1,0:T(8,128)S(1)}, u32[]{:S(2)}, u32[]{:S(2)}) collective-permute-start(f32[32,896]{1,0:T(8,128)S(1)} %reduce_sum.29.after_ref), channel_id=1, source_target_pairs={{0,64},{64,128},{128,192},{192,0},{1,65},{65,129},{129,193},{193,1... | collective-permute-start | bytes 344072 | tf_op jit(solution)/shard_map/ppermute | solution.py:33
  71.5 2.4 %collective-permute-start = (f32[32,896]{1,0:T(8,128)S(1)}, f32[32,896]{1,0:T(8,128)S(1)}, u32[]{:S(2)}, u32[]{:S(2)}) collective-permute-start(f32[32,896]{1,0:T(8,128)S(1)} %reduce_sum.29.after_ref), channel_id=1, source_target_pairs={{0,128},{64,192},{128,0},{192,64},{1,129},{65,193},{129,1},{193,65... | collective-permute-start | bytes 344072 | tf_op jit(solution)/shard_map/ppermute | solution.py:33
  73.9 0.1 transpose.4.low_t_ref
  74.0 0.7 collective-permute-done.2
  74.7 2.8 %collective-permute-done.1 = f32[32,896]{1,0:T(8,128)S(1)} collective-permute-done((f32[32,896]{1,0:T(8,128)S(1)}, f32[32,896]{1,0:T(8,128)S(1)}, u32[]{:S(2)}, u32[]{:S(2)}) %collective-permute-start.1) | collective-permute-done | bytes 114720 | tf_op jit(solution)/shard_map/ppermute | solution.py:33
  77.5 3.8 %collective-permute-done = f32[32,896]{1,0:T(8,128)S(1)} collective-permute-done((f32[32,896]{1,0:T(8,128)S(1)}, f32[32,896]{1,0:T(8,128)S(1)}, u32[]{:S(2)}, u32[]{:S(2)}) %collective-permute-start) | collective-permute-done | bytes 114720 | tf_op jit(solution)/shard_map/ppermute | solution.py:33
  81.3 0.1 broadcast_in_dim.8
  81.3 17.7 %all_to_all.29.total_ref = f32[8,32,896]{2,1,0:T(8,128)S(1)} all-to-all(f32[8,32,896]{2,1,0:T(8,128)S(1)} %broadcast_in_dim.8), channel_id=1, replica_groups=mesh['zh'=4,'zl'=2,'x'=4,'y'=4,'c'=2] {'zl','x'}, dimensions={0} | all-to-all | bytes 1835008 | tf_op jit(solution)/shard_map/all_to_all | solution.py:39
  99.0 3.3 %feedback.1 = (f32[64,3584]{1,0:T(8,128)}, bf16[512,3584]{1,0:T(8,128)(2,1)}) custom-call(f32[8,32,896]{2,1,0:T(8,128)S(1)} %all_to_all.29.total_ref, bf16[512,64]{1,0:T(8,128)(2,1)S(1)} %transpose.4.low_t_ref, bf16[2,512,896]{2,1,0:T(8,128)(2,1)S(1)} %get-tuple-element.14.early_ref, bf16[2,512,896]{2,1,0:T(8,128)(2,1)} %get-tuple-element.15.late_hbm), custom_call_target="tpu_custom_call" | custom-call | tf_op jit(solution)/shard_map/feedback/pallas_call | solution.py:281
  (6 shorter events, 0.1 us)
Async XLA Ops:
  67.3 7.4 %collective-permute-start.2 = (f32[32,896]{1,0:T(8,128)S(1)}, f32[32,896]{1,0:T(8,128)S(1)}, u32[]{:S(2)}, u32[]{:S(2)}) collective-permute-start(f32[32,896]{1,0:T(8,128)S(1)} %reduce_sum.29.after_ref), channel_id=1, source_target_pairs={{0,192},{64,0},{128,64},{192,128},{1,193},{65,1},{129,65},{193,129... | collective-permute-start | bytes 344072 | tf_op jit(solution)/shard_map/ppermute | solution.py:33
  69.2 8.2 %collective-permute-start.1 = (f32[32,896]{1,0:T(8,128)S(1)}, f32[32,896]{1,0:T(8,128)S(1)}, u32[]{:S(2)}, u32[]{:S(2)}) collective-permute-start(f32[32,896]{1,0:T(8,128)S(1)} %reduce_sum.29.after_ref), channel_id=1, source_target_pairs={{0,64},{64,128},{128,192},{192,0},{1,65},{65,129},{129,193},{193,1... | collective-permute-start | bytes 344072 | tf_op jit(solution)/shard_map/ppermute | solution.py:33
  71.5 9.8 %collective-permute-start = (f32[32,896]{1,0:T(8,128)S(1)}, f32[32,896]{1,0:T(8,128)S(1)}, u32[]{:S(2)}, u32[]{:S(2)}) collective-permute-start(f32[32,896]{1,0:T(8,128)S(1)} %reduce_sum.29.after_ref), channel_id=1, source_target_pairs={{0,128},{64,192},{128,0},{192,64},{1,129},{65,193},{129,1},{193,65... | collective-permute-start | bytes 344072 | tf_op jit(solution)/shard_map/ppermute | solution.py:33

commit v7 on v6

--- a/solution.py
+++ b/solution.py
@@ -9,8 +9,8 @@
 from jax.sharding import PartitionSpec as P
 
 SIZES = dict(zh=4, zl=2, x=4, y=4, c=2)
-FIRST = ("zl", "x", "c")
-REST = ("zh", "y")
+PLANE = ("x", "y", "c")
+LINE = ("zh", "zl")
 NEAR = ("zl", "x")
 REPLICAS = SIZES["zh"] * SIZES["zl"] * SIZES["x"]
 QUARTERS = SIZES["x"]
@@ -40,11 +40,9 @@
 
 
 def sum_all(tiles):
-    members = math.prod(SIZES[a] for a in FIRST)
-    parts = lax.all_to_all(tiles, FIRST, 0, 0, tiled=True)
-    piece = jnp.sum(parts.reshape((members, -1) + tiles.shape[1:]), 0)
-    piece = jnp.sum(copies(piece, REST), 0)
-    return copies(piece, FIRST).reshape(tiles.shape)
+    parts = lax.all_to_all(tiles, PLANE, 0, 0, tiled=True)
+    parts = copies(jnp.sum(parts, 0), LINE)
+    return copies(jnp.sum(parts, 0), PLANE)
 
 
 def corrected_kernel(

time: 103 us -> 103 us (level)
  blocking collectives: 74.6 us -> 73.5 us
    all_to_all x3, blocking collectives: 45.4 us -> 41.2 us  [copies(): return lax.all_to_all(sent, axes, 0, 0, tiled=True)]
    all_to_all x1, blocking collectives: 12.3 us -> 15 us  [sum_all(): parts = lax.all_to_all(tiles, PLANE, 0, 0, tiled=True)]
where the time goes in v7:
time: 103 us
  blocking collectives  73.5 us (71%)
  Pallas kernels  13 us (13%)
  waiting for transfers between devices  8.17 us (8%)
  starting transfers between devices  7.08 us (7%)
    all_to_all x3, blocking collectives, copies(): return lax.all_to_all(sent, axes, 0, 0, tiled=True)  41.2 us
    all_to_all x1, blocking collectives, local(): block = jnp.sum(lax.all_to_all(terms, NEAR, 0, 0, tiled=True), 0)  17.3 us
    all_to_all x1, blocking collectives, sum_all(): parts = lax.all_to_all(tiles, PLANE, 0, 0, tiled=True)  15 us
    ppermute x3, waiting for transfers between devices, shift(): return lax.ppermute(block, axis, [(i, (i + step) % n) for i in range(n)])  8.17 us
    ppermute x3, starting transfers between devices, shift(): return lax.ppermute(block, axis, [(i, (i + step) % n) for i in range(n)])  7.08 us
    pallas_call x1, Pallas kernels, corrected_and_factor(): pl.pallas_call(corrected_kernel, in_specs=[pl.BlockSpec(memory_space=pltp...  5.43 us
    pallas_call x1, Pallas kernels, factor_and_terms(): pl.pallas_call(factor_kernel, in_specs=[whole, whole, pl.BlockSpec(memory...  4.14 us
    pallas_call x1, Pallas kernels, finish(): pl.pallas_call(feedback_kernel, in_specs=[whole, whole, whole, hbm], out_...  3.33 us
  transfers between devices with their start and end apart: 3, of which 3 were waited for; matrix products, arithmetic and copies ran while one was open for 0% of the time, Pallas kernels for 0%

profile of v7, /device:TPU:64, one launch (start us, length us, event | category | flops | bytes accessed | tf_op | source)
XLA Modules:
  0.0 102.6 jit_solution(12282801351567101880)
XLA Ops:
  0.6 5.4 %corrected.1 = (bf16[2,512,896]{2,1,0:T(8,128)(2,1)S(1)}, bf16[2,512,896]{2,1,0:T(8,128)(2,1)}, f32[32,8,128]{2,1,0:T(8,128)S(1)}) custom-call(bf16[256,512]{1,0:T(8,128)(2,1)} %x_hbm.1, bf16[256,3584]{1,0:T(8,128)(2,1)} %g_hbm.1, bf16[512,3584]{1,0:T(8,128)(2,1)} %fb_hbm.1, f32[64,3584]{1,0:T(8,128)} %basis_hbm.1), custom_call_target="tpu_custom_call" | custom-call | tf_op jit(solution)/shard_map/corrected/pallas_call | solution.py:109
  6.1 15.0 %all_to_all.25 = f32[32,8,128]{2,1,0:T(8,128)S(1)} all-to-all(f32[32,8,128]{2,1,0:T(8,128)S(1)} %get-tuple-element.13), channel_id=1, replica_groups=mesh['zh'=4,'zl'=2,'x'=4,'y'=4,'c'=2] {'x','y','c'}, dimensions={0} | all-to-all | bytes 262144 | tf_op jit(solution)/shard_map/all_to_all | solution.py:43
  21.1 13.4 %all_to_all.26 = f32[8,8,128]{2,1,0:T(8,128)S(1)} all-to-all(f32[8,8,128]{2,1,0:T(8,128)S(1)} %broadcast_in_dim.6), channel_id=1, replica_groups=mesh['zh'=4,'zl'=2,'x'=4,'y'=4,'c'=2] {'zh','zl'}, dimensions={0} | all-to-all | bytes 65536 | tf_op jit(solution)/shard_map/all_to_all | solution.py:39
  34.6 11.3 %all_to_all.27.tiles_ref = f32[32,8,128]{2,1,0:T(8,128)S(1)} all-to-all(f32[32,8,128]{2,1,0:T(8,128)S(1)} %broadcast_in_dim.7), channel_id=1, replica_groups=mesh['zh'=4,'zl'=2,'x'=4,'y'=4,'c'=2] {'x','y','c'}, dimensions={0} | all-to-all | bytes 262144 | tf_op jit(solution)/shard_map/all_to_all | solution.py:39
  45.8 4.1 %factor.1 = (f32[64,512]{1,0:T(8,128)}, bf16[64,512]{1,0:T(8,128)(2,1)S(1)}, f32[8,32,896]{2,1,0:T(8,128)S(1)}) custom-call(f32[32,8,128]{2,1,0:T(8,128)S(1)} %all_to_all.27.tiles_ref, bf16[2,512,896]{2,1,0:T(8,128)(2,1)S(1)} %get-tuple-element.14.early_ref, bf16[2,512,896]{2,1,0:T(8,128)(2,1)} %get-tuple-element.15.late_hbm), custom_call_target="tpu_custom_call" | custom-call | tf_op jit(solution)/shard_map/factor/pallas_call | solution.py:213
  50.0 17.3 %all_to_all.28 = f32[8,32,896]{2,1,0:T(8,128)S(1)} all-to-all(f32[8,32,896]{2,1,0:T(8,128)S(1)} %get-tuple-element.17), channel_id=1, replica_groups=mesh['zh'=4,'zl'=2,'x'=4,'y'=4,'c'=2] {'zl','x'}, dimensions={0} | all-to-all | bytes 1835008 | tf_op jit(solution)/shard_map/all_to_all | solution.py:304
  67.3 2.6 %collective-permute-start.2 = (f32[32,896]{1,0:T(8,128)S(1)}, f32[32,896]{1,0:T(8,128)S(1)}, u32[]{:S(2)}, u32[]{:S(2)}) collective-permute-start(f32[32,896]{1,0:T(8,128)S(1)} %reduce_sum.29.after_ref), channel_id=1, source_target_pairs={{0,192},{64,0},{128,64},{192,128},{1,193},{65,1},{129,65},{193,129... | collective-permute-start | bytes 344072 | tf_op jit(solution)/shard_map/ppermute | solution.py:33
  69.9 1.6 %collective-permute-start.1 = (f32[32,896]{1,0:T(8,128)S(1)}, f32[32,896]{1,0:T(8,128)S(1)}, u32[]{:S(2)}, u32[]{:S(2)}) collective-permute-start(f32[32,896]{1,0:T(8,128)S(1)} %reduce_sum.29.after_ref), channel_id=1, source_target_pairs={{0,64},{64,128},{128,192},{192,0},{1,65},{65,129},{129,193},{193,1... | collective-permute-start | bytes 344072 | tf_op jit(solution)/shard_map/ppermute | solution.py:33
  71.5 2.9 %collective-permute-start = (f32[32,896]{1,0:T(8,128)S(1)}, f32[32,896]{1,0:T(8,128)S(1)}, u32[]{:S(2)}, u32[]{:S(2)}) collective-permute-start(f32[32,896]{1,0:T(8,128)S(1)} %reduce_sum.29.after_ref), channel_id=1, source_target_pairs={{0,128},{64,192},{128,0},{192,64},{1,129},{65,193},{129,1},{193,65... | collective-permute-start | bytes 344072 | tf_op jit(solution)/shard_map/ppermute | solution.py:33
  74.4 0.1 transpose.4.low_t_ref
  74.5 3.0 %collective-permute-done.2 = f32[32,896]{1,0:T(8,128)S(1)} collective-permute-done((f32[32,896]{1,0:T(8,128)S(1)}, f32[32,896]{1,0:T(8,128)S(1)}, u32[]{:S(2)}, u32[]{:S(2)}) %collective-permute-start.2) | collective-permute-done | bytes 114720 | tf_op jit(solution)/shard_map/ppermute | solution.py:33
  77.4 1.1 %collective-permute-done.1 = f32[32,896]{1,0:T(8,128)S(1)} collective-permute-done((f32[32,896]{1,0:T(8,128)S(1)}, f32[32,896]{1,0:T(8,128)S(1)}, u32[]{:S(2)}, u32[]{:S(2)}) %collective-permute-start.1) | collective-permute-done | bytes 114720 | tf_op jit(solution)/shard_map/ppermute | solution.py:33
  78.6 4.1 %collective-permute-done = f32[32,896]{1,0:T(8,128)S(1)} collective-permute-done((f32[32,896]{1,0:T(8,128)S(1)}, f32[32,896]{1,0:T(8,128)S(1)}, u32[]{:S(2)}, u32[]{:S(2)}) %collective-permute-start) | collective-permute-done | bytes 114720 | tf_op jit(solution)/shard_map/ppermute | solution.py:33
  82.7 0.1 broadcast_in_dim.8
  82.8 16.5 %all_to_all.29.total_ref = f32[8,32,896]{2,1,0:T(8,128)S(1)} all-to-all(f32[8,32,896]{2,1,0:T(8,128)S(1)} %broadcast_in_dim.8), channel_id=1, replica_groups=mesh['zh'=4,'zl'=2,'x'=4,'y'=4,'c'=2] {'zl','x'}, dimensions={0} | all-to-all | bytes 1835008 | tf_op jit(solution)/shard_map/all_to_all | solution.py:39
  99.3 3.3 %feedback.1 = (f32[64,3584]{1,0:T(8,128)}, bf16[512,3584]{1,0:T(8,128)(2,1)}) custom-call(f32[8,32,896]{2,1,0:T(8,128)S(1)} %all_to_all.29.total_ref, bf16[512,64]{1,0:T(8,128)(2,1)S(1)} %transpose.4.low_t_ref, bf16[2,512,896]{2,1,0:T(8,128)(2,1)S(1)} %get-tuple-element.14.early_ref, bf16[2,512,896]{2,1,0:T(8,128)(2,1)} %get-tuple-element.15.late_hbm), custom_call_target="tpu_custom_call" | custom-call | tf_op jit(solution)/shard_map/feedback/pallas_call | solution.py:279
  (6 shorter events, 0.1 us)
Async XLA Ops:
  67.3 10.2 %collective-permute-start.2 = (f32[32,896]{1,0:T(8,128)S(1)}, f32[32,896]{1,0:T(8,128)S(1)}, u32[]{:S(2)}, u32[]{:S(2)}) collective-permute-start(f32[32,896]{1,0:T(8,128)S(1)} %reduce_sum.29.after_ref), channel_id=1, source_target_pairs={{0,192},{64,0},{128,64},{192,128},{1,193},{65,1},{129,65},{193,129... | collective-permute-start | bytes 344072 | tf_op jit(solution)/shard_map/ppermute | solution.py:33
  69.9 8.7 %collective-permute-start.1 = (f32[32,896]{1,0:T(8,128)S(1)}, f32[32,896]{1,0:T(8,128)S(1)}, u32[]{:S(2)}, u32[]{:S(2)}) collective-permute-start(f32[32,896]{1,0:T(8,128)S(1)} %reduce_sum.29.after_ref), channel_id=1, source_target_pairs={{0,64},{64,128},{128,192},{192,0},{1,65},{65,129},{129,193},{193,1... | collective-permute-start | bytes 344072 | tf_op jit(solution)/shard_map/ppermute | solution.py:33
  71.5 11.2 %collective-permute-start = (f32[32,896]{1,0:T(8,128)S(1)}, f32[32,896]{1,0:T(8,128)S(1)}, u32[]{:S(2)}, u32[]{:S(2)}) collective-permute-start(f32[32,896]{1,0:T(8,128)S(1)} %reduce_sum.29.after_ref), channel_id=1, source_target_pairs={{0,128},{64,192},{128,0},{192,64},{1,129},{65,193},{129,1},{193,65... | collective-permute-start | bytes 344072 | tf_op jit(solution)/shard_map/ppermute | solution.py:33
